TPU v7x, 32 devices: a whole 2x2x4 slice. The times are simulated.
32 devices in a mesh: vox: 16 (over z, x, core), echo: 2 (over y).
Axes of the slice: x: 2, y: 2, z: 4, core: 2. Of those that a mesh axis runs over, the one named last changes fastest.
Arguments:
- acquired: bfloat16 [131072, 128], P(('vox', 'echo')), may hold values from -6 to 6
- owner: int32 [131072, 1], P(('vox', 'echo')), may hold values from 0 to 15; in each aligned block of 4096 rows (0 to 4095, 4096 to 8191, ...) at most 1024 rows name the same one
- slot: int32 [131072, 1], P(('vox', 'echo')), may hold values from 0 to 32767
- sampled: int32 [4096, 256], P('vox', 'echo'), may hold values 0 or 1
- left_panel: bfloat16 [128, 32], replicated, may hold values from -0.5 to 0.5
- right_panel: bfloat16 [256, 32], P('echo'), may hold values from -0.75 to 0.75
Outputs:
- coefficients: bfloat16 [4096, 1024], P(('vox', 'echo'))
Inputs may be any that keep to these rules, and one draw needn't show every extreme that they name: Among the rows of one device, no owner is named more than 1024 times, a bound that some block reaches.
All inputs are finite; a program needn't handle non-finite values. No bound on the sum of `sampled` on one device may be relied on, other than what follows from the above.
Results may differ from a plain program's by a relative error of at most 0.005.
Values may be sent and summed in bfloat16 or wider, within the bound.
No kernel may reach another device: no remote copies, remote signals or barrier semaphores. Data moves between devices by JAX's collectives and lax.ppermute only.
A program may use at most 64 MiB of HBM per device.

v0:
```python
import jax
import jax.numpy as jnp
from jax import lax
from jax.sharding import PartitionSpec as P


def on_device(acquired, owner, slot, sampled, left_panel, right_panel):
    owners = lax.axis_size("vox")
    row_count = acquired.shape[0]
    capacity = 4 * row_count // owners
    vox_local, echo_local = sampled.shape
    rank_width = left_panel.shape[1]
    target = owner[:, 0]
    owner_hot = (target[:, None] == jnp.arange(owners, dtype=jnp.int32)[None, :]).astype(jnp.int32)
    position = jnp.sum(jnp.cumsum(owner_hot, axis=0) * owner_hot, axis=1) - 1
    reduced = jnp.dot(acquired, left_panel, preferred_element_type=jnp.float32).astype(jnp.bfloat16)
    send_block = min(1024, row_count)
    send_turns = row_count // send_block
    owner_blocks = owner_hot.reshape(send_turns, send_block, owners)
    place_blocks = position.reshape(send_turns, send_block)
    reduced_blocks = reduced.reshape(send_turns, send_block, rank_width)
    label_blocks = (slot[:, 0] + 1).astype(jnp.float32).reshape(send_turns, send_block)
    cap_range = jnp.arange(capacity, dtype=jnp.int32)

    def pack_rows(carry, pieces):
        buffer_sum, label_sum = carry
        owner_piece, place_piece, reduced_piece, label_piece = pieces
        place_hot = place_piece[:, None] == cap_range[None, :]
        spread = owner_piece.astype(jnp.bfloat16)[:, :, None] * reduced_piece[:, None, :]
        buffer_sum = buffer_sum + jnp.einsum(
            "ip,ior->opr",
            place_hot.astype(jnp.bfloat16),
            spread,
            preferred_element_type=jnp.float32,
        )
        labelled = owner_piece.astype(jnp.float32) * label_piece[:, None]
        label_sum = label_sum + jnp.einsum(
            "ip,io->op", place_hot.astype(jnp.float32), labelled, precision=lax.Precision.HIGHEST
        )
        return ((buffer_sum, label_sum), None)

    start_carry = (
        jnp.zeros((owners, capacity, rank_width), jnp.float32),
        jnp.zeros((owners, capacity), jnp.float32),
    )
    (buffer_sum, label_sum), _ = lax.scan(
        pack_rows, start_carry, (owner_blocks, place_blocks, reduced_blocks, label_blocks)
    )
    buffer = buffer_sum.astype(jnp.bfloat16)
    slot_ids = label_sum.astype(jnp.int32) - 1
    arrived, arrived_ids = (
        lax.all_to_all(buffer, "vox", split_axis=0, concat_axis=0, tiled=True),
        lax.all_to_all(slot_ids, "vox", split_axis=0, concat_axis=0, tiled=True),
    )
    arrived_count = owners * capacity
    take_block = min(1024, arrived_count)
    take_turns = arrived_count // take_block
    arrived_blocks = arrived.reshape(take_turns, take_block, rank_width)
    id_blocks = arrived_ids.reshape(take_turns, take_block)
    vox_range = jnp.arange(vox_local, dtype=jnp.int32)
    echo_range = jnp.arange(echo_local, dtype=jnp.int32)

    def fill_rows(total, pieces):
        row_piece, id_piece = pieces
        voxel_hot = (id_piece[:, None] // echo_local == vox_range[None, :]) & (
            id_piece[:, None] >= 0
        )
        echo_hot = id_piece[:, None] % echo_local == echo_range[None, :]
        spread = echo_hot.astype(jnp.bfloat16)[:, :, None] * row_piece[:, None, :]
        total = total + jnp.einsum(
            "iv,ier->ver",
            voxel_hot.astype(jnp.bfloat16),
            spread,
            preferred_element_type=jnp.float32,
        )
        return (total, None)

    filled, _ = lax.scan(
        fill_rows,
        jnp.zeros((vox_local, echo_local, rank_width), jnp.float32),
        (arrived_blocks, id_blocks),
    )
    filled = filled * sampled.astype(jnp.float32)[:, :, None]
    partial_core = jnp.einsum(
        "ver,es->vrs", filled, right_panel.astype(jnp.float32), precision=lax.Precision.HIGHEST
    )
    partial_core = partial_core.reshape(vox_local, rank_width * rank_width)
    total = lax.psum(partial_core, "echo")
    share = vox_local // lax.axis_size("echo")
    result = lax.dynamic_slice_in_dim(total, lax.axis_index("echo") * share, share, 0)
    return result.astype(jnp.bfloat16)


def solution(mesh):
    return jax.shard_map(
        on_device,
        mesh=mesh,
        in_specs=(
            P(("vox", "echo"), None),
            P(("vox", "echo"), None),
            P(("vox", "echo"), None),
            P("vox", "echo"),
            P(),
            P("echo", None),
        ),
        out_specs=P(("vox", "echo"), None),
        check_vma=False,
    )
```

profile of v0, /device:TPU:0, one launch (start us, length us, event | category | flops | bytes accessed | tf_op | source)
XLA Modules:
  0.0 251.0 jit_solution(16615414940940144799)
XLA Ops:
  0.0 1.5 fusion.43
  1.5 8.3 %reduce-window.6 = s32[16,32,128]{2,1,0:T(8,128)S(1)} reduce-window(s32[16,32,128]{2,1,0:T(8,128)} %fusion.43, s32[]{:T(128)} %constant.87.clone.1), window={size=1x1x128 pad=0_0x0_0x127_0}, to_apply=%region_0.0 | reduce-window | flops 8323072 | bytes 524292 | tf_op jit(solution)/shard_map/reduce-window
  9.8 0.5 slice_reduce_fusion
  10.6 0.9 fusion.41
  11.6 1.2 convolution_convert_fusion
  12.7 0.5 broadcast.207
  13.3 1.4 reduce.9
  14.7 0.7 fusion.42
  15.5 23.1 %while.26 = (s32[]{:T(128)}, f32[16,1024,32]{1,2,0:T(8,128)S(1)}, f32[16,1024]{1,0:T(8,128)}, s32[4,1024,16]{1,2,0:T(8,128)}, bf16[4,1024,32]{1,2,0:T(8,128)(2,1...) while((s32[]{:T(128)}, f32[16,1024,32]{1,2,0:T(8,128)S(1)}, ...), condition=%wide.region_4.5_spmd.clone, body=%wide.region_3.4_spmd.clone.sunk | while | flops 1278820352 | bytes 4747896 | solution.py:46
  15.5 0.8 fusion.56
  16.4 1.9 bitcast_add_fusion.2
  18.3 2.9 %fusion.57 = f32[16,1024]{1,0:T(8,128)} fusion(s32[1024]{0:T(1024)S(1)} %bitcast.82, f32[16,1024]{1,0:T(8,128)} %get-tuple-element.304, s32[4,1024,16]{1,2,0:T(8,128)} %get-tuple-element.314, s32[]{:T(128)} %get-tuple-element.302, f32[1024]{0:T(1024)S(1)} %bitcast.83, pred[]{:T(512)S(6)} %compare.20), kind=kOutput, calls=%fused_computation.10.clone.1 | convolution fusion | flops 202440704 | bytes 205313 | tf_op jit(solution)/shard_map/while/body/eval_jaxpr/ip,io->op/dot_general | solution.py:37
  21.2 0.8 fusion.56
  22.1 1.9 bitcast_add_fusion.2
  24.0 3.0 %fusion.57 = f32[16,1024]{1,0:T(8,128)} fusion(s32[1024]{0:T(1024)S(1)} %bitcast.82, f32[16,1024]{1,0:T(8,128)} %get-tuple-element.304, s32[4,1024,16]{1,2,0:T(8,128)} %get-tuple-element.314, s32[]{:T(128)} %get-tuple-element.302, f32[1024]{0:T(1024)S(1)} %bitcast.83, pred[]{:T(512)S(6)} %compare.20), kind=kOutput, calls=%fused_computation.10.clone.1 | convolution fusion | flops 202440704 | bytes 205313 | tf_op jit(solution)/shard_map/while/body/eval_jaxpr/ip,io->op/dot_general | solution.py:37
  27.0 0.8 fusion.56
  27.9 1.9 bitcast_add_fusion.2
  29.8 3.0 %fusion.57 = f32[16,1024]{1,0:T(8,128)} fusion(s32[1024]{0:T(1024)S(1)} %bitcast.82, f32[16,1024]{1,0:T(8,128)} %get-tuple-element.304, s32[4,1024,16]{1,2,0:T(8,128)} %get-tuple-element.314, s32[]{:T(128)} %get-tuple-element.302, f32[1024]{0:T(1024)S(1)} %bitcast.83, pred[]{:T(512)S(6)} %compare.20), kind=kOutput, calls=%fused_computation.10.clone.1 | convolution fusion | flops 202440704 | bytes 205313 | tf_op jit(solution)/shard_map/while/body/eval_jaxpr/ip,io->op/dot_general | solution.py:37
  32.8 0.8 fusion.56
  33.7 1.9 bitcast_add_fusion.2
  35.6 3.0 %fusion.57 = f32[16,1024]{1,0:T(8,128)} fusion(s32[1024]{0:T(1024)S(1)} %bitcast.82, f32[16,1024]{1,0:T(8,128)} %get-tuple-element.304, s32[4,1024,16]{1,2,0:T(8,128)} %get-tuple-element.314, s32[]{:T(128)} %get-tuple-element.302, f32[1024]{0:T(1024)S(1)} %bitcast.83, pred[]{:T(512)S(6)} %compare.20), kind=kOutput, calls=%fused_computation.10.clone.1 | convolution fusion | flops 202440704 | bytes 205313 | tf_op jit(solution)/shard_map/while/body/eval_jaxpr/ip,io->op/dot_general | solution.py:37
  38.6 0.9 convert_add_fusion
  39.4 0.7 all_to_all.11
  40.1 7.4 %all-to-all-start = ((s32[16,1,1024]{2,1,0:T(1,128)}), s32[16,1,1024]{2,1,0:T(1,128)S(1)}, u32[]{:S(2)}, u32[]{:S(2)}) async-start(s32[16,1,1024]{2,1,0:T(1,128)} %all_to_all.11), calls=%async_computation | async-start | bytes 131072 | tf_op jit(solution)/shard_map/all_to_all | solution.py:53
  47.5 1.1 convert_element_type.66
  48.6 5.8 %all-to-all-done = s32[16,1,1024]{2,1,0:T(1,128)S(1)} async-done(((s32[16,1,1024]{2,1,0:T(1,128)}), s32[16,1,1024]{2,1,0:T(1,128)S(1)}, u32[]{:S(2)}, u32[]{:S(2)}) %all-to-all-start) | async-done | bytes 65568 | tf_op jit(solution)/shard_map/all_to_all | solution.py:53
  54.4 3.7 %all-to-all-start.1 = ((bf16[16,1024,32]{1,2,0:T(8,128)(2,1)}), bf16[16,1024,32]{1,2,0:T(8,128)(2,1)S(1)}, u32[]{:S(2)}, u32[]{:S(2)}) async-start(bf16[16,1024,32]{1,2,0:T(8,128)(2,1)} %convert_element_type.66), calls=%async_computation.1 | async-start | bytes 2097152 | tf_op jit(solution)/shard_map/all_to_all | solution.py:52
  58.1 22.8 %all-to-all-done.1 = bf16[16,1024,32]{1,2,0:T(8,128)(2,1)S(1)} async-done(((bf16[16,1024,32]{1,2,0:T(8,128)(2,1)}), bf16[16,1024,32]{1,2,0:T(8,128)(2,1)S(1)}, u32[]{:S(2)}, u32[]{:S(2)}) %all-to-all-start.1) | async-done | bytes 1048608 | tf_op jit(solution)/shard_map/all_to_all | solution.py:52
  81.0 133.5 %while.27 = (s32[]{:T(128)}, f32[256,128,32]{1,0,2:T(8,128)}, s32[16,1024]{1,0:T(8,128)S(1)}, bf16[16,1024,32]{1,2,0:T(8,128)(2,1)S(1)}, s32[]{:T(128)}, /*index=5*/s32[]{:T(128)}) while((s32[]{:T(128)}, f32[256,128,32]{1,0,2:T(8,128)}, s32[16,1024]{1,0:T(8,128)S(1)}, bf16[16,1024,32]{1,2,0:T(8,128)(2,1)S(1)}, s32[]{:T(128)}, ...), condition=%wide.region_6.7_spmd.clone, body=%wide.region_5.6_spmd.clone.sunk | while | flops 2167164928 | bytes 9144407 | solution.py:78
  81.2 6.8 %select_add_fusion.2 = f32[256,128,32]{1,0,2:T(8,128)} fusion(f32[256,128,32]{1,0,2:T(8,128)} %get-tuple-element.327, pred[]{:T(512)S(6)} %compare.21, bf16[1024,32]{0,1:T(8,128)(2,1)S(1)} %dynamic-slice_bitcast_fusion.5, bf16[1024,128]{1,0:T(8,128)(2,1)S(1)} %fusion.60, s32[1024]{0:T(1024)S(1)} %get-tuple-element.292, ...), kind=kOutput, calls=%fused_computation.26.clone.1 | convolution fusion | flops 2166882304 | bytes 8721409 | tf_op jit(solution)/shard_map/while/body/eval_jaxpr/iv,ier->ver/dot_general | solution.py:70
  88.3 8.2 %select_add_fusion.2 = f32[256,128,32]{1,0,2:T(8,128)} fusion(f32[256,128,32]{1,0,2:T(8,128)} %get-tuple-element.327, pred[]{:T(512)S(6)} %compare.21, bf16[1024,32]{0,1:T(8,128)(2,1)S(1)} %dynamic-slice_bitcast_fusion.5, bf16[1024,128]{1,0:T(8,128)(2,1)S(1)} %fusion.60, s32[1024]{0:T(1024)S(1)} %get-tuple-element.292, ...), kind=kOutput, calls=%fused_computation.26.clone.1 | convolution fusion | flops 2166882304 | bytes 8721409 | tf_op jit(solution)/shard_map/while/body/eval_jaxpr/iv,ier->ver/dot_general | solution.py:70
  96.7 8.2 %select_add_fusion.2 = f32[256,128,32]{1,0,2:T(8,128)} fusion(f32[256,128,32]{1,0,2:T(8,128)} %get-tuple-element.327, pred[]{:T(512)S(6)} %compare.21, bf16[1024,32]{0,1:T(8,128)(2,1)S(1)} %dynamic-slice_bitcast_fusion.5, bf16[1024,128]{1,0:T(8,128)(2,1)S(1)} %fusion.60, s32[1024]{0:T(1024)S(1)} %get-tuple-element.292, ...), kind=kOutput, calls=%fused_computation.26.clone.1 | convolution fusion | flops 2166882304 | bytes 8721409 | tf_op jit(solution)/shard_map/while/body/eval_jaxpr/iv,ier->ver/dot_general | solution.py:70
  105.1 8.2 %select_add_fusion.2 = f32[256,128,32]{1,0,2:T(8,128)} fusion(f32[256,128,32]{1,0,2:T(8,128)} %get-tuple-element.327, pred[]{:T(512)S(6)} %compare.21, bf16[1024,32]{0,1:T(8,128)(2,1)S(1)} %dynamic-slice_bitcast_fusion.5, bf16[1024,128]{1,0:T(8,128)(2,1)S(1)} %fusion.60, s32[1024]{0:T(1024)S(1)} %get-tuple-element.292, ...), kind=kOutput, calls=%fused_computation.26.clone.1 | convolution fusion | flops 2166882304 | bytes 8721409 | tf_op jit(solution)/shard_map/while/body/eval_jaxpr/iv,ier->ver/dot_general | solution.py:70
  113.6 8.2 %select_add_fusion.2 = f32[256,128,32]{1,0,2:T(8,128)} fusion(f32[256,128,32]{1,0,2:T(8,128)} %get-tuple-element.327, pred[]{:T(512)S(6)} %compare.21, bf16[1024,32]{0,1:T(8,128)(2,1)S(1)} %dynamic-slice_bitcast_fusion.5, bf16[1024,128]{1,0:T(8,128)(2,1)S(1)} %fusion.60, s32[1024]{0:T(1024)S(1)} %get-tuple-element.292, ...), kind=kOutput, calls=%fused_computation.26.clone.1 | convolution fusion | flops 2166882304 | bytes 8721409 | tf_op jit(solution)/shard_map/while/body/eval_jaxpr/iv,ier->ver/dot_general | solution.py:70
  122.0 8.2 %select_add_fusion.2 = f32[256,128,32]{1,0,2:T(8,128)} fusion(f32[256,128,32]{1,0,2:T(8,128)} %get-tuple-element.327, pred[]{:T(512)S(6)} %compare.21, bf16[1024,32]{0,1:T(8,128)(2,1)S(1)} %dynamic-slice_bitcast_fusion.5, bf16[1024,128]{1,0:T(8,128)(2,1)S(1)} %fusion.60, s32[1024]{0:T(1024)S(1)} %get-tuple-element.292, ...), kind=kOutput, calls=%fused_computation.26.clone.1 | convolution fusion | flops 2166882304 | bytes 8721409 | tf_op jit(solution)/shard_map/while/body/eval_jaxpr/iv,ier->ver/dot_general | solution.py:70
  130.4 8.2 %select_add_fusion.2 = f32[256,128,32]{1,0,2:T(8,128)} fusion(f32[256,128,32]{1,0,2:T(8,128)} %get-tuple-element.327, pred[]{:T(512)S(6)} %compare.21, bf16[1024,32]{0,1:T(8,128)(2,1)S(1)} %dynamic-slice_bitcast_fusion.5, bf16[1024,128]{1,0:T(8,128)(2,1)S(1)} %fusion.60, s32[1024]{0:T(1024)S(1)} %get-tuple-element.292, ...), kind=kOutput, calls=%fused_computation.26.clone.1 | convolution fusion | flops 2166882304 | bytes 8721409 | tf_op jit(solution)/shard_map/while/body/eval_jaxpr/iv,ier->ver/dot_general | solution.py:70
  138.8 8.2 %select_add_fusion.2 = f32[256,128,32]{1,0,2:T(8,128)} fusion(f32[256,128,32]{1,0,2:T(8,128)} %get-tuple-element.327, pred[]{:T(512)S(6)} %compare.21, bf16[1024,32]{0,1:T(8,128)(2,1)S(1)} %dynamic-slice_bitcast_fusion.5, bf16[1024,128]{1,0:T(8,128)(2,1)S(1)} %fusion.60, s32[1024]{0:T(1024)S(1)} %get-tuple-element.292, ...), kind=kOutput, calls=%fused_computation.26.clone.1 | convolution fusion | flops 2166882304 | bytes 8721409 | tf_op jit(solution)/shard_map/while/body/eval_jaxpr/iv,ier->ver/dot_general | solution.py:70
  147.3 8.2 %select_add_fusion.2 = f32[256,128,32]{1,0,2:T(8,128)} fusion(f32[256,128,32]{1,0,2:T(8,128)} %get-tuple-element.327, pred[]{:T(512)S(6)} %compare.21, bf16[1024,32]{0,1:T(8,128)(2,1)S(1)} %dynamic-slice_bitcast_fusion.5, bf16[1024,128]{1,0:T(8,128)(2,1)S(1)} %fusion.60, s32[1024]{0:T(1024)S(1)} %get-tuple-element.292, ...), kind=kOutput, calls=%fused_computation.26.clone.1 | convolution fusion | flops 2166882304 | bytes 8721409 | tf_op jit(solution)/shard_map/while/body/eval_jaxpr/iv,ier->ver/dot_general | solution.py:70
  155.7 8.2 %select_add_fusion.2 = f32[256,128,32]{1,0,2:T(8,128)} fusion(f32[256,128,32]{1,0,2:T(8,128)} %get-tuple-element.327, pred[]{:T(512)S(6)} %compare.21, bf16[1024,32]{0,1:T(8,128)(2,1)S(1)} %dynamic-slice_bitcast_fusion.5, bf16[1024,128]{1,0:T(8,128)(2,1)S(1)} %fusion.60, s32[1024]{0:T(1024)S(1)} %get-tuple-element.292, ...), kind=kOutput, calls=%fused_computation.26.clone.1 | convolution fusion | flops 2166882304 | bytes 8721409 | tf_op jit(solution)/shard_map/while/body/eval_jaxpr/iv,ier->ver/dot_general | solution.py:70
  164.1 8.2 %select_add_fusion.2 = f32[256,128,32]{1,0,2:T(8,128)} fusion(f32[256,128,32]{1,0,2:T(8,128)} %get-tuple-element.327, pred[]{:T(512)S(6)} %compare.21, bf16[1024,32]{0,1:T(8,128)(2,1)S(1)} %dynamic-slice_bitcast_fusion.5, bf16[1024,128]{1,0:T(8,128)(2,1)S(1)} %fusion.60, s32[1024]{0:T(1024)S(1)} %get-tuple-element.292, ...), kind=kOutput, calls=%fused_computation.26.clone.1 | convolution fusion | flops 2166882304 | bytes 8721409 | tf_op jit(solution)/shard_map/while/body/eval_jaxpr/iv,ier->ver/dot_general | solution.py:70
  172.6 8.2 %select_add_fusion.2 = f32[256,128,32]{1,0,2:T(8,128)} fusion(f32[256,128,32]{1,0,2:T(8,128)} %get-tuple-element.327, pred[]{:T(512)S(6)} %compare.21, bf16[1024,32]{0,1:T(8,128)(2,1)S(1)} %dynamic-slice_bitcast_fusion.5, bf16[1024,128]{1,0:T(8,128)(2,1)S(1)} %fusion.60, s32[1024]{0:T(1024)S(1)} %get-tuple-element.292, ...), kind=kOutput, calls=%fused_computation.26.clone.1 | convolution fusion | flops 2166882304 | bytes 8721409 | tf_op jit(solution)/shard_map/while/body/eval_jaxpr/iv,ier->ver/dot_general | solution.py:70
  181.0 8.2 %select_add_fusion.2 = f32[256,128,32]{1,0,2:T(8,128)} fusion(f32[256,128,32]{1,0,2:T(8,128)} %get-tuple-element.327, pred[]{:T(512)S(6)} %compare.21, bf16[1024,32]{0,1:T(8,128)(2,1)S(1)} %dynamic-slice_bitcast_fusion.5, bf16[1024,128]{1,0:T(8,128)(2,1)S(1)} %fusion.60, s32[1024]{0:T(1024)S(1)} %get-tuple-element.292, ...), kind=kOutput, calls=%fused_computation.26.clone.1 | convolution fusion | flops 2166882304 | bytes 8721409 | tf_op jit(solution)/shard_map/while/body/eval_jaxpr/iv,ier->ver/dot_general | solution.py:70
  189.4 8.2 %select_add_fusion.2 = f32[256,128,32]{1,0,2:T(8,128)} fusion(f32[256,128,32]{1,0,2:T(8,128)} %get-tuple-element.327, pred[]{:T(512)S(6)} %compare.21, bf16[1024,32]{0,1:T(8,128)(2,1)S(1)} %dynamic-slice_bitcast_fusion.5, bf16[1024,128]{1,0:T(8,128)(2,1)S(1)} %fusion.60, s32[1024]{0:T(1024)S(1)} %get-tuple-element.292, ...), kind=kOutput, calls=%fused_computation.26.clone.1 | convolution fusion | flops 2166882304 | bytes 8721409 | tf_op jit(solution)/shard_map/while/body/eval_jaxpr/iv,ier->ver/dot_general | solution.py:70
  197.9 8.2 %select_add_fusion.2 = f32[256,128,32]{1,0,2:T(8,128)} fusion(f32[256,128,32]{1,0,2:T(8,128)} %get-tuple-element.327, pred[]{:T(512)S(6)} %compare.21, bf16[1024,32]{0,1:T(8,128)(2,1)S(1)} %dynamic-slice_bitcast_fusion.5, bf16[1024,128]{1,0:T(8,128)(2,1)S(1)} %fusion.60, s32[1024]{0:T(1024)S(1)} %get-tuple-element.292, ...), kind=kOutput, calls=%fused_computation.26.clone.1 | convolution fusion | flops 2166882304 | bytes 8721409 | tf_op jit(solution)/shard_map/while/body/eval_jaxpr/iv,ier->ver/dot_general | solution.py:70
  206.3 8.2 %select_add_fusion.2 = f32[256,128,32]{1,0,2:T(8,128)} fusion(f32[256,128,32]{1,0,2:T(8,128)} %get-tuple-element.327, pred[]{:T(512)S(6)} %compare.21, bf16[1024,32]{0,1:T(8,128)(2,1)S(1)} %dynamic-slice_bitcast_fusion.5, bf16[1024,128]{1,0:T(8,128)(2,1)S(1)} %fusion.60, s32[1024]{0:T(1024)S(1)} %get-tuple-element.292, ...), kind=kOutput, calls=%fused_computation.26.clone.1 | convolution fusion | flops 2166882304 | bytes 8721409 | tf_op jit(solution)/shard_map/while/body/eval_jaxpr/iv,ier->ver/dot_general | solution.py:70
  214.4 4.8 %fusion.37 = f32[256,32,32]{0,2,1:T(8,128)S(1)} fusion(f32[256,128,32]{1,0,2:T(8,128)} %get-tuple-element.130, f32[256,128]{1,0:T(8,128)S(1)} %convert_element_type.67, bf16[128,32]{0,1:T(8,128)(2,1)S(1)} %copy-done.3), kind=kOutput, calls=%fused_computation.48 | convolution fusion | flops 403701760 | bytes 5382144 | tf_op jit(solution)/shard_map/ver,es->vrs/dot_general | solution.py:84
  219.6 30.7 %all-reduce.1 = bf16[256,1024]{1,0:T(8,128)(2,1)S(1)} all-reduce(f32[256,1024]{1,0:T(8,128)S(1)} %copy.12), channel_id=1, replica_groups=mesh['vox'=16,'echo'=2] {'echo'}, use_global_device_ids=true, to_apply=%region_7.8 | all-reduce | flops 262144 | bytes 1572864 | tf_op jit(solution)/shard_map/psum | solution.py:88
  250.2 0.7 dynamic-slice_convert_fusion.1
  (114 shorter events, 4.8 us)
Async XLA Ops:
  0.0 11.6 %copy-start = (bf16[4096,128]{1,0:T(8,128)(2,1)S(1)}, bf16[4096,128]{1,0:T(8,128)(2,1)}, u32[]{:S(2)}) copy-start(bf16[4096,128]{1,0:T(8,128)(2,1)} %param.10) | copy-start | bytes 3145732
  0.0 15.4 %copy-start.2 = (s32[4096,1]{0,1:T(1,128)S(1)}, s32[4096,1]{0,1:T(1,128)}, u32[]{:S(2)}) copy-start(s32[4096,1]{0,1:T(1,128)} %param.12) | copy-start | bytes 49156
  38.6 19.5 %copy-start.1 = (s32[256,128]{1,0:T(8,128)S(1)}, s32[256,128]{1,0:T(8,128)}, u32[]{:S(2)}) copy-start(s32[256,128]{1,0:T(8,128)} %param.13) | copy-start | bytes 393220
  40.1 14.3 %all-to-all-start = ((s32[16,1,1024]{2,1,0:T(1,128)}), s32[16,1,1024]{2,1,0:T(1,128)S(1)}, u32[]{:S(2)}, u32[]{:S(2)}) async-start(s32[16,1,1024]{2,1,0:T(1,128)} %all_to_all.11), calls=%async_computation | async-start | bytes 131072 | tf_op jit(solution)/shard_map/all_to_all | solution.py:53
  54.4 26.6 %all-to-all-start.1 = ((bf16[16,1024,32]{1,2,0:T(8,128)(2,1)}), bf16[16,1024,32]{1,2,0:T(8,128)(2,1)S(1)}, u32[]{:S(2)}, u32[]{:S(2)}) async-start(bf16[16,1024,32]{1,2,0:T(8,128)(2,1)} %convert_element_type.66), calls=%async_computation.1 | async-start | bytes 2097152 | tf_op jit(solution)/shard_map/all_to_all | solution.py:52
  81.0 133.5 %copy-start.3 = (bf16[128,32]{0,1:T(8,128)(2,1)S(1)}, bf16[128,32]{0,1:T(8,128)(2,1)}, u32[]{:S(2)}) copy-start(bf16[128,32]{0,1:T(8,128)(2,1)} %param.15) | copy-start | bytes 24580
where the time goes:
time: 254 us; the launch traced here: 251 us
  matrix products  154 us (61%)
  blocking collectives  30.7 us (12%)
  waiting for transfers between devices  28.6 us (11%)
  other arithmetic  22.1 us (9%)
  starting transfers between devices  11 us (4%)
  local copies, waits for them, and re-layouts  3.26 us (1%)
    dot_general x16, matrix products, fill_rows(): jnp.einsum('iv,ier->ver', voxel_hot.astype(jnp.bfloat16), spread, preferr...  129 us
    psum x1, blocking collectives, on_device(): total = lax.psum(partial_core, 'echo')  30.7 us
    all_to_all x1, waiting for transfers between devices, on_device(): lax.all_to_all(buffer, 'vox', split_axis=0, concat_axis=0, tiled=True)  22.8 us
    dot_general x4, matrix products, pack_rows(): jnp.einsum('ip,io->op', place_hot.astype(jnp.float32), labelled, precisio...  11.9 us
    another operation x3, other arithmetic  8.62 us
    dot_general x4, matrix products, pack_rows(): jnp.einsum('ip,ior->opr', place_hot.astype(jnp.bfloat16), spread, preferr...  7.56 us
    all_to_all x1, starting transfers between devices, on_device(): lax.all_to_all(slot_ids, 'vox', split_axis=0, concat_axis=0, tiled=True)  7.37 us
    all_to_all x1, waiting for transfers between devices, on_device(): lax.all_to_all(slot_ids, 'vox', split_axis=0, concat_axis=0, tiled=True)  5.76 us
  transfers between devices with their start and end apart: 2, of which 2 were waited for; matrix products, arithmetic and copies ran while one was open for 0% of the time, Pallas kernels for 0%

commit v1 on v0

v1 whole, which is shorter than its diff:
```python
import functools

import jax
import jax.numpy as jnp
from jax import lax
from jax.experimental import pallas as pl
from jax.experimental.pallas import tpu as pltpu
from jax.sharding import PartitionSpec as P

LANES = 128
CHUNK = 512
FINE = 16
BF16 = jnp.bfloat16
F32 = jnp.float32
I32 = jnp.int32


def nt_dot(lhs, rhs):
    return lax.dot_general(
        lhs, rhs, (((1,), (1,)), ((), ())), preferred_element_type=F32
    )


def nn_dot(lhs, rhs):
    return lax.dot_general(
        lhs, rhs, (((1,), (0,)), ((), ())), preferred_element_type=F32
    )


def pack_kernel(
    owners, capacity, echo_local, me_ref, acquired_ref, owner_ref, slot_ref, left_ref,
    out_ref, place_ref, feature_ref, id_ref,
):
    rows = acquired_ref.shape[0]
    rank = left_ref.shape[0]
    chunks = rows // CHUNK
    groups = capacity // LANES
    me = me_ref[0]
    owner_range = lax.broadcasted_iota(I32, (owners, CHUNK), 0)
    hots = []
    for j in range(chunks):
        relative = owner_ref[:, j * CHUNK : (j + 1) * CHUNK] ^ me
        hots.append((owner_range == relative).astype(F32))
    hot = jnp.concatenate(hots, axis=0)
    before = lax.broadcasted_iota(I32, (CHUNK, CHUNK), 0) < lax.broadcasted_iota(
        I32, (CHUNK, CHUNK), 1
    )
    prefix = nn_dot(hot.astype(BF16), before.astype(F32).astype(BF16))
    carry = jnp.zeros((owners, 1), F32)
    for j in range(chunks):
        part = prefix[j * owners : (j + 1) * owners]
        place = jnp.sum((part + carry) * hots[j], axis=0, keepdims=True)
        place_ref[j] = place.astype(I32)
        carry = carry + jnp.sum(hots[j], axis=1, keepdims=True)
    feature_ref[...] = jnp.zeros_like(feature_ref)
    id_ref[...] = jnp.zeros_like(id_ref)
    left = left_ref[...]
    lane_range = lax.broadcasted_iota(I32, (LANES, CHUNK), 0)
    group_range = lax.broadcasted_iota(I32, (8, CHUNK), 0)

    def step(j, _):
        at = pl.multiple_of(j * CHUNK, CHUNK)
        reduced = nt_dot(left, acquired_ref[pl.ds(at, CHUNK), :]).astype(BF16)
        relative = owner_ref[:, pl.ds(at, CHUNK)] ^ me
        slot = slot_ref[:, pl.ds(at, CHUNK)]
        place = place_ref[j]
        group = place // LANES
        lane_hot = (lane_range == place % LANES).astype(F32).astype(BF16)
        group_b = jnp.broadcast_to(group.astype(F32), (LANES, CHUNK)).astype(BF16)
        place_hot = jnp.concatenate(
            [
                jnp.where(group_b == BF16(g), lane_hot, BF16(0))
                for g in range(groups)
            ],
            axis=0,
        )
        here = group_range == group
        voxel = jnp.where(here, (slot // echo_local).astype(F32), 0.0)
        echo = jnp.where(here, (slot % echo_local).astype(F32), 0.0)
        ids = jnp.concatenate([voxel, echo], axis=0).astype(BF16)
        owner_b = jnp.broadcast_to(relative.astype(F32), (rank, CHUNK)).astype(BF16)
        owner_c = owner_b[:16]
        spread = jnp.concatenate(
            [jnp.where(owner_b == BF16(o), reduced, BF16(0)) for o in range(owners)],
            axis=0,
        )
        spread_ids = jnp.concatenate(
            [jnp.where(owner_c == BF16(o), ids, BF16(0)) for o in range(owners)],
            axis=0,
        )
        feature_ref[...] += nt_dot(spread, place_hot)
        id_ref[...] += nt_dot(spread_ids, lane_hot)
        return 0

    lax.fori_loop(0, chunks, step, 0)
    for o in range(owners):
        for g in range(groups):
            out_ref[o, g * rank : (g + 1) * rank, :] = feature_ref[
                o * rank : (o + 1) * rank, g * LANES : (g + 1) * LANES
            ].astype(BF16)
        out_ref[o, groups * rank :, :] = id_ref[o * 16 : (o + 1) * 16, :].astype(BF16)


def core_kernel(groups, blocks_ref, sampled_ref, right_ref, out_ref, a_ref, b_ref):
    count = blocks_ref.shape[0]
    rank = right_ref.shape[0]
    shares, _, width = out_ref.shape
    echo_local = sampled_ref.shape[1]
    bits = sampled_ref[0:32, :]
    for b in range(1, sampled_ref.shape[0] // 32):
        bits = bits + (sampled_ref[b * 32 : (b + 1) * 32, :] << b)
    table = jnp.concatenate([right_ref[...], bits.astype(F32).astype(BF16)], axis=0)
    echo_range = lax.broadcasted_iota(I32, (echo_local, LANES), 0).astype(F32).astype(BF16)
    bit_range = lax.broadcasted_iota(I32, (32, LANES), 0)
    out_ref[...] = jnp.zeros_like(out_ref)

    def step(s, _):
        ids = blocks_ref[s, groups * rank :, :].astype(F32)
        for g in range(groups):
            feature = blocks_ref[s, g * rank : (g + 1) * rank, :]
            voxel = ids[g : g + 1].astype(I32)
            echo = jnp.broadcast_to(ids[8 + g : 9 + g], (echo_local, LANES)).astype(BF16)
            echo_hot = jnp.where(echo == echo_range, BF16(1), BF16(0))
            found = nn_dot(table, echo_hot)
            word = jnp.sum(
                jnp.where(bit_range == voxel % 32, found[rank:], 0.0),
                axis=0, keepdims=True,
            ).astype(I32)
            mask = ((word >> (voxel // 32)) & 1).astype(F32)
            right = (found[:rank] * mask).astype(BF16)
            low = jnp.broadcast_to((voxel % FINE).astype(F32), (rank, LANES)).astype(BF16)
            high = jnp.broadcast_to((voxel // FINE).astype(F32), (rank, LANES)).astype(BF16)
            at = slice(g * LANES, (g + 1) * LANES)
            for v in range(FINE):
                a_ref[v * rank : (v + 1) * rank, at] = jnp.where(
                    low == BF16(v), feature, BF16(0)
                )
                b_ref[v * rank : (v + 1) * rank, at] = jnp.where(
                    high == BF16(v), right, BF16(0)
                )
        for h in range(shares):
            out_ref[h] += nt_dot(a_ref[...], b_ref[h * width : (h + 1) * width, :])
        return 0

    lax.fori_loop(0, count, step, 0)


def finish_kernel(rank, keep_ref, got_ref, out_ref, sum_ref):
    tiles = keep_ref.shape[1] // LANES
    per = LANES // rank
    block = lax.broadcasted_iota(I32, (FINE, LANES), 1) // rank
    for t in range(tiles):
        sum_ref[...] = (
            keep_ref[:, t * LANES : (t + 1) * LANES]
            + got_ref[:, t * LANES : (t + 1) * LANES].astype(F32)
        )
        for q in range(rank // per):
            rows = [
                sum_ref[pl.ds(q * per + i, FINE, stride=rank), :] for i in range(per)
            ]
            for k in range(per):
                made = None
                for i in range(per):
                    turn = (i - k) % per * rank
                    moved = pltpu.roll(rows[i], turn, 1) if turn else rows[i]
                    made = moved if made is None else jnp.where(block == i, moved, made)
                v = t * per + k
                out_ref[v * FINE : (v + 1) * FINE, q * LANES : (q + 1) * LANES] = (
                    made.astype(BF16)
                )


VMEM = pl.BlockSpec(memory_space=pltpu.VMEM)
SMEM = pl.BlockSpec(memory_space=pltpu.SMEM)
PARAMS = pltpu.CompilerParams(vmem_limit_bytes=48 * 2**20)


def on_device(acquired, owner, slot, sampled, left_panel, right_panel):
    owners = lax.axis_size("vox")
    shares = lax.axis_size("echo")
    rows = acquired.shape[0]
    capacity = 4 * rows // owners
    groups = capacity // LANES
    vox_local, echo_local = sampled.shape
    rank = left_panel.shape[1]
    depth = groups * rank + 16
    width = FINE * rank // shares
    packed = pl.pallas_call(
        functools.partial(pack_kernel, owners, capacity, echo_local),
        out_shape=jax.ShapeDtypeStruct((owners, depth, LANES), BF16),
        in_specs=[SMEM, VMEM, VMEM, VMEM, VMEM],
        out_specs=VMEM,
        scratch_shapes=[
            pltpu.VMEM((rows // CHUNK, 1, CHUNK), I32),
            pltpu.VMEM((owners * rank, capacity), F32),
            pltpu.VMEM((owners * 16, LANES), F32),
        ],
        compiler_params=PARAMS,
        name="pack",
    )(
        jnp.zeros((1,), I32),
        acquired,
        owner.reshape(1, rows),
        slot.reshape(1, rows),
        left_panel.T,
    )
    arrived = lax.all_to_all(packed, "vox", split_axis=0, concat_axis=0, tiled=True)
    core = pl.pallas_call(
        functools.partial(core_kernel, groups),
        out_shape=jax.ShapeDtypeStruct((shares, FINE * rank, width), F32),
        in_specs=[VMEM, VMEM, VMEM],
        out_specs=VMEM,
        scratch_shapes=[
            pltpu.VMEM((FINE * rank, capacity), BF16),
            pltpu.VMEM((FINE * rank, capacity), BF16),
        ],
        compiler_params=PARAMS,
        name="core",
    )(arrived, sampled, right_panel.T)
    share = vox_local // shares
    if shares != 2 or width % LANES:
        total = lax.psum_scatter(core, "echo", scatter_dimension=0)
        total = total.reshape(FINE, rank, width // rank, rank).transpose(2, 0, 1, 3)
        return total.reshape(share, rank * rank).astype(BF16)
    mine = lax.axis_index("echo")
    keep = lax.dynamic_index_in_dim(core, mine, 0, keepdims=False)
    give = lax.dynamic_index_in_dim(core, 1 - mine, 0, keepdims=False).astype(BF16)
    got = lax.ppermute(give, "echo", [(0, 1), (1, 0)])
    return pl.pallas_call(
        functools.partial(finish_kernel, rank),
        out_shape=jax.ShapeDtypeStruct((share, rank * rank), BF16),
        in_specs=[VMEM, VMEM],
        out_specs=VMEM,
        scratch_shapes=[pltpu.VMEM((FINE * rank, LANES), F32)],
        compiler_params=PARAMS,
        name="finish",
    )(keep, got)


def solution(mesh):
    return jax.shard_map(
        on_device,
        mesh=mesh,
        in_specs=(
            P(("vox", "echo"), None),
            P(("vox", "echo"), None),
            P(("vox", "echo"), None),
            P("vox", "echo"),
            P(),
            P("echo", None),
        ),
        out_specs=P(("vox", "echo"), None),
        check_vma=False,
    )
```

time: 254 us -> 70.4 us (0.28)
  matrix products: 154 us -> 0 us
  blocking collectives: 30.7 us -> 0 us
  Pallas kernels: 0 us -> 25.3 us
  other arithmetic: 22.1 us -> 0 us
  waiting for transfers between devices: 28.6 us -> 31.4 us
    dot_general x26 -> x0, matrix products: 154 us -> none  [the longest x16 129 us: fill_rows(): jnp.einsum('iv,ier->ver', voxel_hot.astype(jnp.bfloat16), spread, preferr...]
    psum x1 -> x0, blocking collectives: 30.7 us -> none  [on_device(): total = lax.psum(partial_core, 'echo')]
    pallas_call x0 -> x3, Pallas kernels: none -> 25.3 us  [the longest x1 15.4 us: on_device(): pl.pallas_call(functools.partial(core_kernel, groups), out_shape=jax.Shap...]
    convert_element_type x25 -> x0, other arithmetic: 10.1 us -> none  [the longest x4 3.38 us: pack_rows(): owner_piece.astype(jnp.bfloat16)[:, :, None] * reduced_piece[:, None, :]]
    another operation x3 -> x0, other arithmetic: 8.62 us -> none
    ppermute x0 -> x1, waiting for transfers between devices: none -> 7.39 us  [on_device(): got = lax.ppermute(give, 'echo', [(0, 1), (1, 0)])]
    all_to_all x2 -> x1, waiting for transfers between devices: 28.6 us -> 24 us  [on_device(): lax.all_to_all(packed, 'vox', split_axis=0, concat_axis=0, tiled=True)]
    all_to_all x2 -> x1, starting transfers between devices: 11 us -> 7.49 us  [on_device(): lax.all_to_all(packed, 'vox', split_axis=0, concat_axis=0, tiled=True)]
where the time goes in v1:
time: 70.4 us; the launch traced here: 69.3 us
  waiting for transfers between devices  31.4 us (45%)
  Pallas kernels  25.3 us (36%)
  starting transfers between devices  9.07 us (13%)
  local copies, waits for them, and re-layouts  3.43 us (5%)
    all_to_all x1, waiting for transfers between devices, on_device(): lax.all_to_all(packed, 'vox', split_axis=0, concat_axis=0, tiled=True)  24 us
    pallas_call x1, Pallas kernels, on_device(): pl.pallas_call(functools.partial(core_kernel, groups), out_shape=jax.Shap...  15.4 us
    pallas_call x1, Pallas kernels, on_device(): pl.pallas_call(functools.partial(pack_kernel, owners, capacity, echo_loca...  8.8 us
    all_to_all x1, starting transfers between devices, on_device(): lax.all_to_all(packed, 'vox', split_axis=0, concat_axis=0, tiled=True)  7.49 us
    ppermute x1, waiting for transfers between devices, on_device(): got = lax.ppermute(give, 'echo', [(0, 1), (1, 0)])  7.39 us
    unnamed x12, local copies, waits for them, and re-layouts  3.36 us
    ppermute x1, starting transfers between devices, on_device(): got = lax.ppermute(give, 'echo', [(0, 1), (1, 0)])  1.58 us
  transfers between devices with their start and end apart: 2, of which 2 were waited for; matrix products, arithmetic and copies ran while one was open for 0% of the time, Pallas kernels for 0%

profile of v1, /device:TPU:0, one launch (start us, length us, event | category | flops | bytes accessed | tf_op | source)
XLA Modules:
  0.0 69.3 jit_solution(16254357770231247040)
XLA Ops:
  0.0 0.0 copy-start
  0.0 1.2 %copy-done = bf16[4096,128]{1,0:T(8,128)(2,1)S(1)} copy-done((bf16[4096,128]{1,0:T(8,128)(2,1)S(1)}, bf16[4096,128]{1,0:T(8,128)(2,1)}, u32[]{:S(2)}) %copy-start) | copy-done | bytes 1048600
  1.2 0.0 copy-start.2
  1.2 0.7 %copy-done.2 = s32[4096,1]{0,1:T(1,128)S(1)} copy-done((s32[4096,1]{0,1:T(1,128)S(1)}, s32[4096,1]{0,1:T(1,128)}, u32[]{:S(2)}) %copy-start.2) | copy-done | bytes 16408
  1.9 0.0 copy-start.3
  1.9 0.7 %copy-done.3 = s32[4096,1]{0,1:T(1,128)S(1)} copy-done((s32[4096,1]{0,1:T(1,128)S(1)}, s32[4096,1]{0,1:T(1,128)}, u32[]{:S(2)}) %copy-start.3) | copy-done | bytes 16408
  2.7 0.0 copy-start.4
  2.7 0.7 %copy-done.4 = bf16[128,32]{0,1:T(8,128)(2,1)S(1)} copy-done((bf16[128,32]{0,1:T(8,128)(2,1)S(1)}, bf16[128,32]{0,1:T(8,128)(2,1)}, u32[]{:S(2)}) %copy-start.4) | copy-done | bytes 8216
  3.4 8.8 %pack.1 = bf16[16,272,128]{2,1,0:T(8,128)(2,1)} custom-call(s32[1]{0:T(128)} %constant.12.clone.1.me_ref, bf16[4096,128]{1,0:T(8,128)(2,1)S(1)} %copy-done, s32[1,4096]{1,0:T(1,128)S(1)} %bitcast.8, s32[1,4096]{1,0:T(1,128)S(1)} %bitcast.9, bf16[32,128]{1,0:T(8,128)(2,1)S(1)} %bitcast.10), custom_call_target="tpu_custom_call" | custom-call | tf_op jit(solution)/shard_map/pack/pallas_call | solution.py:188
  12.2 0.0 copy-start.1
  12.2 0.0 copy-start.5
  12.2 7.5 %all-to-all-start = ((bf16[16,272,128]{2,1,0:T(8,128)(2,1)}), bf16[16,272,128]{2,1,0:T(8,128)(2,1)S(1)}, u32[]{:S(2)}, u32[]{:S(2)}) async-start(bf16[16,272,128]{2,1,0:T(8,128)(2,1)} %pack.1), calls=%async_computation | async-start | bytes 2228224 | tf_op jit(solution)/shard_map/all_to_all | solution.py:207
  19.7 24.0 %all-to-all-done.blocks_ref = bf16[16,272,128]{2,1,0:T(8,128)(2,1)S(1)} async-done(((bf16[16,272,128]{2,1,0:T(8,128)(2,1)}), bf16[16,272,128]{2,1,0:T(8,128)(2,1)S(1)}, u32[]{:S(2)}, u32[]{:S(2)}) %all-to-all-start) | async-done | bytes 1114144 | tf_op jit(solution)/shard_map/all_to_all | solution.py:207
  43.7 0.0 copy-done.1
  43.7 0.0 copy-done.5
  43.7 15.4 %core.1 = f32[2,512,256]{2,1,0:T(8,128)S(1)} custom-call(bf16[16,272,128]{2,1,0:T(8,128)(2,1)S(1)} %all-to-all-done.blocks_ref, s32[256,128]{1,0:T(8,128)S(1)} %copy-done.1, bf16[32,128]{1,0:T(8,128)(2,1)S(1)} %bitcast.11), custom_call_target="tpu_custom_call" | custom-call | tf_op jit(solution)/shard_map/core/pallas_call | solution.py:208
  59.1 1.6 %collective-permute-start = (bf16[512,256]{1,0:T(8,128)(2,1)S(1)}, bf16[512,256]{1,0:T(8,128)(2,1)S(1)}, u32[]{:S(2)}, u32[]{:S(2)}) collective-permute-start(bf16[512,256]{1,0:T(8,128)(2,1)S(1)} %fusion), channel_id=1, source_target_pairs={{0,1},{1,0},{2,3},{3,2},{4,5},{5,4},{6,7},{7,6},{8,9},{9,8},{10,11... | collective-permute-start | bytes 786440 | tf_op jit(solution)/shard_map/ppermute | solution.py:228
  60.7 7.4 %collective-permute-done.got_ref = bf16[512,256]{1,0:T(8,128)(2,1)S(1)} collective-permute-done((bf16[512,256]{1,0:T(8,128)(2,1)S(1)}, bf16[512,256]{1,0:T(8,128)(2,1)S(1)}, u32[]{:S(2)}, u32[]{:S(2)}) %collective-permute-start) | collective-permute-done | bytes 262176 | tf_op jit(solution)/shard_map/ppermute | solution.py:228
  68.1 1.2 %finish.1 = bf16[128,1024]{1,0:T(8,128)(2,1)} custom-call(f32[512,256]{1,0:T(8,128)S(1)} %dynamic-slice_bitcast_fusion.keep_ref, bf16[512,256]{1,0:T(8,128)(2,1)S(1)} %collective-permute-done.got_ref), custom_call_target="tpu_custom_call" | custom-call | tf_op jit(solution)/shard_map/finish/pallas_call | solution.py:229
  (2 shorter events, 0.1 us)
Async XLA Ops:
  0.0 1.2 %copy-start = (bf16[4096,128]{1,0:T(8,128)(2,1)S(1)}, bf16[4096,128]{1,0:T(8,128)(2,1)}, u32[]{:S(2)}) copy-start(bf16[4096,128]{1,0:T(8,128)(2,1)} %acquired_ref.1) | copy-start | bytes 3145732
  1.2 0.7 %copy-start.2 = (s32[4096,1]{0,1:T(1,128)S(1)}, s32[4096,1]{0,1:T(1,128)}, u32[]{:S(2)}) copy-start(s32[4096,1]{0,1:T(1,128)} %param.7) | copy-start | bytes 49156
  1.9 0.7 %copy-start.3 = (s32[4096,1]{0,1:T(1,128)S(1)}, s32[4096,1]{0,1:T(1,128)}, u32[]{:S(2)}) copy-start(s32[4096,1]{0,1:T(1,128)} %param.8) | copy-start | bytes 49156
  2.7 0.7 %copy-start.4 = (bf16[128,32]{0,1:T(8,128)(2,1)S(1)}, bf16[128,32]{0,1:T(8,128)(2,1)}, u32[]{:S(2)}) copy-start(bf16[128,32]{0,1:T(8,128)(2,1)} %param.10) | copy-start | bytes 24580
  12.2 31.5 %copy-start.1 = (s32[256,128]{1,0:T(8,128)S(1)}, s32[256,128]{1,0:T(8,128)}, u32[]{:S(2)}) copy-start(s32[256,128]{1,0:T(8,128)} %sampled_ref.1) | copy-start | bytes 393220
  12.2 31.5 %copy-start.5 = (bf16[128,32]{0,1:T(8,128)(2,1)S(1)}, bf16[128,32]{0,1:T(8,128)(2,1)}, u32[]{:S(2)}) copy-start(bf16[128,32]{0,1:T(8,128)(2,1)} %param.11) | copy-start | bytes 24580
  12.2 31.5 %all-to-all-start = ((bf16[16,272,128]{2,1,0:T(8,128)(2,1)}), bf16[16,272,128]{2,1,0:T(8,128)(2,1)S(1)}, u32[]{:S(2)}, u32[]{:S(2)}) async-start(bf16[16,272,128]{2,1,0:T(8,128)(2,1)} %pack.1), calls=%async_computation | async-start | bytes 2228224 | tf_op jit(solution)/shard_map/all_to_all | solution.py:207
  59.1 9.0 %collective-permute-start = (bf16[512,256]{1,0:T(8,128)(2,1)S(1)}, bf16[512,256]{1,0:T(8,128)(2,1)S(1)}, u32[]{:S(2)}, u32[]{:S(2)}) collective-permute-start(bf16[512,256]{1,0:T(8,128)(2,1)S(1)} %fusion), channel_id=1, source_target_pairs={{0,1},{1,0},{2,3},{3,2},{4,5},{5,4},{6,7},{7,6},{8,9},{9,8},{10,11... | collective-permute-start | bytes 786440 | tf_op jit(solution)/shard_map/ppermute | solution.py:228

commit v2 on v1

v2 whole, which is shorter than its diff:
```python
import functools

import jax
import jax.numpy as jnp
from jax import lax
from jax.experimental import pallas as pl
from jax.experimental.pallas import tpu as pltpu
from jax.sharding import PartitionSpec as P

LANES = 128
CHUNK = 512
FINE = 16
BF16 = jnp.bfloat16
F32 = jnp.float32
I32 = jnp.int32


def nt_dot(lhs, rhs):
    return lax.dot_general(
        lhs, rhs, (((1,), (1,)), ((), ())), preferred_element_type=F32
    )


def nn_dot(lhs, rhs):
    return lax.dot_general(
        lhs, rhs, (((1,), (0,)), ((), ())), preferred_element_type=F32
    )


def place_rows(owners, me, owner_ref, place_ref):
    rows = owner_ref.shape[1]
    chunks = rows // CHUNK
    owner_range = lax.broadcasted_iota(I32, (owners, CHUNK), 0)
    hots = []
    for j in range(chunks):
        relative = owner_ref[:, j * CHUNK : (j + 1) * CHUNK] ^ me
        hots.append((owner_range == relative).astype(F32))
    hot = jnp.concatenate(hots, axis=0)
    before = lax.broadcasted_iota(I32, (CHUNK, CHUNK), 0) < lax.broadcasted_iota(
        I32, (CHUNK, CHUNK), 1
    )
    prefix = nn_dot(hot.astype(BF16), before.astype(F32).astype(BF16))
    carry = jnp.zeros((owners, 1), F32)
    for j in range(chunks):
        part = prefix[j * owners : (j + 1) * owners]
        place = jnp.sum((part + carry) * hots[j], axis=0, keepdims=True)
        place_ref[j] = place.astype(I32)
        carry = carry + jnp.sum(hots[j], axis=1, keepdims=True)


def put_rows(
    first, capacity, echo_local, me, reduced_ref, owner_ref, slot_ref, place_ref,
    out_refs, feature_ref, id_ref,
):
    rank, rows = reduced_ref.shape
    count = len(out_refs)
    groups = capacity // LANES
    lane_range = lax.broadcasted_iota(I32, (LANES, CHUNK), 0)
    group_range = lax.broadcasted_iota(I32, (8, CHUNK), 0)

    def step(j, _):
        at = pl.multiple_of(j * CHUNK, CHUNK)
        reduced = reduced_ref[:, pl.ds(at, CHUNK)]
        relative = owner_ref[:, pl.ds(at, CHUNK)] ^ me
        slot = slot_ref[:, pl.ds(at, CHUNK)]
        place = place_ref[j]
        group = place // LANES
        lane_hot = (lane_range == place % LANES).astype(F32).astype(BF16)
        group_b = jnp.broadcast_to(group.astype(F32), (LANES, CHUNK)).astype(BF16)
        place_hot = jnp.concatenate(
            [
                jnp.where(group_b == BF16(g), lane_hot, BF16(0))
                for g in range(groups)
            ],
            axis=0,
        )
        here = group_range == group
        voxel = jnp.where(here, (slot // echo_local).astype(F32), 0.0)
        echo = jnp.where(here, (slot % echo_local).astype(F32), 0.0)
        ids = jnp.concatenate([voxel, echo], axis=0).astype(BF16)
        owner_b = jnp.broadcast_to(relative.astype(F32), (rank, CHUNK)).astype(BF16)
        owner_c = owner_b[:16]
        spread = jnp.concatenate(
            [
                jnp.where(owner_b == BF16(first + o), reduced, BF16(0))
                for o in range(count)
            ],
            axis=0,
        )
        spread_ids = jnp.concatenate(
            [
                jnp.where(owner_c == BF16(first + o), ids, BF16(0))
                for o in range(count)
            ],
            axis=0,
        )
        feature = nt_dot(spread, place_hot)
        id_sum = nt_dot(spread_ids, lane_hot)

        @pl.when(j == 0)
        def _():
            feature_ref[...] = feature
            id_ref[...] = id_sum

        @pl.when(j > 0)
        def _():
            feature_ref[...] += feature
            id_ref[...] += id_sum

        return 0

    lax.fori_loop(0, rows // CHUNK, step, 0)
    for o in range(count):
        for g in range(groups):
            out_refs[o][g * rank : (g + 1) * rank, :] = feature_ref[
                o * rank : (o + 1) * rank, g * LANES : (g + 1) * LANES
            ].astype(BF16)
        out_refs[o][groups * rank :, :] = id_ref[o * 16 : (o + 1) * 16, :].astype(BF16)


def far_kernel(
    owners, capacity, echo_local, me_ref, acquired_hbm, owner_hbm, slot_hbm, left_ref,
    reduced_ref, place_ref, *refs,
):
    outs = refs[: owners // 2]
    acquired_ref, owner_ref, slot_ref, feature_ref, id_ref, sems = refs[owners // 2 :]
    copies = [
        pltpu.make_async_copy(a, b, sems.at[i])
        for i, (a, b) in enumerate(
            [(owner_hbm, owner_ref), (slot_hbm, slot_ref), (acquired_hbm, acquired_ref)]
        )
    ]
    for copy in copies:
        copy.start()
    copies[0].wait()
    me = me_ref[0]
    place_rows(owners, me, owner_ref, place_ref)
    copies[1].wait()
    copies[2].wait()
    reduced_ref[...] = nt_dot(left_ref[...], acquired_ref[...]).astype(BF16)
    put_rows(
        owners // 2, capacity, echo_local, me, reduced_ref, owner_ref, slot_ref, place_ref,
        outs, feature_ref, id_ref,
    )


def near_kernel(
    owners, capacity, echo_local, me_ref, owner_ref, slot_ref, reduced_ref, place_ref, *refs
):
    put_rows(
        0, capacity, echo_local, me_ref[0], reduced_ref, owner_ref, slot_ref, place_ref,
        refs[: owners // 2], *refs[owners // 2 :],
    )


def core_kernel(count, halves, more, flip_ref, sampled_ref, right_ref, *refs):
    blocks, refs = refs[:count], refs[count:]
    before = refs[: len(halves)] if more else None
    refs = refs[len(halves) :] if more else refs
    outs, (a_ref, b_ref) = refs[: len(halves)], refs[len(halves) :]
    rank = right_ref.shape[0]
    groups = (blocks[0].shape[0] - 16) // rank
    size = groups * LANES
    half = FINE // 2
    flip = flip_ref[0] * half
    echo_local = sampled_ref.shape[1]
    bits = sampled_ref[0:32, :]
    for b in range(1, sampled_ref.shape[0] // 32):
        bits = bits + (sampled_ref[b * 32 : (b + 1) * 32, :] << b)
    table = jnp.concatenate([right_ref[...], bits.astype(F32).astype(BF16)], axis=0)
    echo_range = lax.broadcasted_iota(I32, (echo_local, LANES), 0).astype(F32).astype(BF16)
    bit_range = lax.broadcasted_iota(I32, (32, LANES), 0)
    for s, block in enumerate(blocks):
        ids = block[groups * rank :, :].astype(F32)
        for g in range(groups):
            feature = block[g * rank : (g + 1) * rank, :]
            voxel = ids[g : g + 1].astype(I32)
            echo = jnp.broadcast_to(ids[8 + g : 9 + g], (echo_local, LANES)).astype(BF16)
            echo_hot = jnp.where(echo == echo_range, BF16(1), BF16(0))
            found = nn_dot(table, echo_hot)
            word = jnp.sum(
                jnp.where(bit_range == voxel % 32, found[rank:], 0.0),
                axis=0, keepdims=True,
            ).astype(I32)
            mask = ((word >> (voxel // 32)) & 1).astype(F32)
            right = (found[:rank] * mask).astype(BF16)
            low = (voxel % FINE).astype(F32)
            high = ((voxel // FINE) ^ flip).astype(F32)
            low = jnp.broadcast_to(low, (rank, LANES)).astype(BF16)
            high = jnp.broadcast_to(high, (rank, LANES)).astype(BF16)
            at = slice(s * size + g * LANES, s * size + (g + 1) * LANES)
            for v in range(FINE):
                a_ref[v * rank : (v + 1) * rank, at] = jnp.where(
                    low == BF16(v), feature, BF16(0)
                )
            for h in halves:
                for v in range(half * h, half * (h + 1)):
                    w = v - half * halves[0]
                    b_ref[w * rank : (w + 1) * rank, at] = jnp.where(
                        high == BF16(v), right, BF16(0)
                    )
    for i in range(len(halves)):
        total = nt_dot(a_ref[...], b_ref[i * half * rank : (i + 1) * half * rank, :])
        if more:
            total = total + before[i][...]
        outs[i][...] = total.astype(outs[i].dtype)


def finish_kernel(rank, keep_ref, got_ref, out_ref, sum_ref):
    tiles = keep_ref.shape[1] // LANES
    per = LANES // rank
    block = lax.broadcasted_iota(I32, (FINE, LANES), 1) // rank
    for t in range(tiles):
        sum_ref[...] = (
            keep_ref[:, t * LANES : (t + 1) * LANES]
            + got_ref[:, t * LANES : (t + 1) * LANES].astype(F32)
        )
        for q in range(rank // per):
            rows = [
                sum_ref[pl.ds(q * per + i, FINE, stride=rank), :] for i in range(per)
            ]
            for k in range(per):
                made = None
                for i in range(per):
                    turn = (i - k) % per * rank
                    moved = pltpu.roll(rows[i], turn, 1) if turn else rows[i]
                    made = moved if made is None else jnp.where(block == i, moved, made)
                v = t * per + k
                out_ref[v * FINE : (v + 1) * FINE, q * LANES : (q + 1) * LANES] = (
                    made.astype(BF16)
                )


VMEM = pl.BlockSpec(memory_space=pltpu.VMEM)
SMEM = pl.BlockSpec(memory_space=pltpu.SMEM)
ANY = pl.BlockSpec(memory_space=pl.ANY)
PARAMS = pltpu.CompilerParams(vmem_limit_bytes=40 * 2**20)


def core_call(blocks, flip, sampled, right, halves=(0, 1), before=(), kinds=None):
    rank = right.shape[0]
    groups = (blocks[0].shape[0] - 16) // rank
    rows = len(blocks) * groups * LANES
    wide, narrow = FINE * rank, FINE * rank // 2
    first = 3 + len(blocks)
    kinds = kinds or [F32] * len(halves)
    return pl.pallas_call(
        functools.partial(core_kernel, len(blocks), halves, bool(before)),
        out_shape=[jax.ShapeDtypeStruct((wide, narrow), kind) for kind in kinds],
        in_specs=[SMEM] + [VMEM] * (2 + len(blocks) + len(before)),
        out_specs=[VMEM] * len(halves),
        scratch_shapes=[
            pltpu.VMEM((wide, rows), BF16),
            pltpu.VMEM((narrow * len(halves), rows), BF16),
        ],
        input_output_aliases={
            first + i: i for i in range(len(before)) if kinds[i] == F32
        },
        compiler_params=PARAMS,
        cost_estimate=pl.CostEstimate(
            flops=2 * rows * wide * narrow * len(halves),
            bytes_accessed=rows * 68 + 4 * wide * narrow * len(halves),
            transcendentals=0,
        ),
        name="core",
    )(flip, sampled, right, *blocks, *before)


def on_device(acquired, owner, slot, sampled, left_panel, right_panel):
    owners = lax.axis_size("vox")
    shares = lax.axis_size("echo")
    rows = acquired.shape[0]
    capacity = 4 * rows // owners
    groups = capacity // LANES
    vox_local, echo_local = sampled.shape
    rank = left_panel.shape[1]
    depth = groups * rank + 16
    half = owners // 2
    me = lax.axis_index("vox").reshape(1)
    mine = lax.axis_index("echo")
    owner, slot = owner.reshape(1, rows), slot.reshape(1, rows)
    left, right = left_panel.T, right_panel.T
    block = jax.ShapeDtypeStruct((depth, LANES), BF16)
    sums = [
        pltpu.VMEM((half * rank, capacity), F32),
        pltpu.VMEM((half * 16, LANES), F32),
    ]
    cost = pl.CostEstimate(
        flops=2 * rows * capacity * half * rank,
        bytes_accessed=4 * rows * 128,
        transcendentals=0,
    )
    reduced, place, *far = pl.pallas_call(
        functools.partial(far_kernel, owners, capacity, echo_local),
        out_shape=[
            jax.ShapeDtypeStruct((rank, rows), BF16),
            jax.ShapeDtypeStruct((rows // CHUNK, 1, CHUNK), I32),
        ]
        + [block] * half,
        in_specs=[SMEM, ANY, ANY, ANY, VMEM],
        out_specs=[VMEM] * (2 + half),
        scratch_shapes=[
            pltpu.VMEM(acquired.shape, BF16),
            pltpu.VMEM(owner.shape, I32),
            pltpu.VMEM(slot.shape, I32),
            *sums,
            pltpu.SemaphoreType.DMA((3,)),
        ],
        compiler_params=PARAMS,
        cost_estimate=cost,
        name="far",
    )(me, acquired, owner, slot, left)
    near = pl.pallas_call(
        functools.partial(near_kernel, owners, capacity, echo_local),
        out_shape=[block] * half,
        in_specs=[SMEM] + [VMEM] * 4,
        out_specs=[VMEM] * half,
        scratch_shapes=sums,
        compiler_params=PARAMS,
        cost_estimate=cost,
        name="near",
    )(me, owner, slot, reduced, place)

    def sent(array, mask):
        return lax.ppermute(array, "vox", [(i, i ^ mask) for i in range(owners)])

    order = [*range(half, owners, 2), *range(half + 1, owners, 2)]
    arrived = {m: sent(far[m - half], m) for m in order}
    arrived.update({m: sent(near[m], m) if m else near[0] for m in range(half)})
    two = shares == 2
    flip = ((1 - mine) if two else jnp.zeros((), I32)).astype(I32).reshape(1)
    run = functools.partial(core_call, flip=flip, sampled=sampled, right=right)
    total = run([arrived[m] for m in range(half)])
    late = order[-2:]
    done = order[:-2]
    for i in range(0, len(done), 4):
        total = run([arrived[m] for m in done[i : i + 4]], before=total)
    last = [arrived[m] for m in late]
    share = vox_local // shares
    if not two:
        both = jnp.concatenate(run(last, before=total), axis=1)
        both = both.reshape(FINE * rank, shares, FINE * rank // shares)
        both = lax.psum_scatter(both, "echo", scatter_dimension=1)
        both = both.reshape(FINE, rank, FINE // shares, rank).transpose(2, 0, 1, 3)
        return both.reshape(share, rank * rank).astype(BF16)
    (give,) = run(last, halves=(0,), before=total[:1], kinds=[BF16])
    got = lax.ppermute(give, "echo", [(0, 1), (1, 0)])
    (keep,) = run(last, halves=(1,), before=total[1:])
    return pl.pallas_call(
        functools.partial(finish_kernel, rank),
        out_shape=jax.ShapeDtypeStruct((share, rank * rank), BF16),
        in_specs=[VMEM, VMEM],
        out_specs=VMEM,
        scratch_shapes=[pltpu.VMEM((FINE * rank, LANES), F32)],
        compiler_params=PARAMS,
        name="finish",
    )(keep, got)


def solution(mesh):
    return jax.shard_map(
        on_device,
        mesh=mesh,
        in_specs=(
            P(("vox", "echo"), None),
            P(("vox", "echo"), None),
            P(("vox", "echo"), None),
            P("vox", "echo"),
            P(),
            P("echo", None),
        ),
        out_specs=P(("vox", "echo"), None),
        check_vma=False,
    )
```

time: 70.4 us -> 64.6 us (0.918); the launches traced: 69.3 us -> 64.2 us
  waiting for transfers between devices: 31.4 us -> 13.5 us
  starting transfers between devices: 9.07 us -> 23.2 us
  Pallas kernels: 25.3 us -> 24 us
    all_to_all x1 -> x0, waiting for transfers between devices: 24 us -> none  [on_device(): lax.all_to_all(packed, 'vox', split_axis=0, concat_axis=0, tiled=True)]
    ppermute x0 -> x15, starting transfers between devices: none -> 21.6 us  [sent(): return lax.ppermute(array, 'vox', [(i, i ^ mask) for i in range(owners)])]
    ppermute x0 -> x15, waiting for transfers between devices: none -> 7.87 us  [sent(): return lax.ppermute(array, 'vox', [(i, i ^ mask) for i in range(owners)])]
    all_to_all x1 -> x0, starting transfers between devices: 7.49 us -> none  [on_device(): lax.all_to_all(packed, 'vox', split_axis=0, concat_axis=0, tiled=True)]
    ppermute x1, waiting for transfers between devices: 7.39 us -> 5.63 us  [on_device(): got = lax.ppermute(give, 'echo', [(0, 1), (1, 0)])]
    pallas_call x2 -> x7, Pallas kernels: 24.2 us -> 22.8 us  [the longest x5 12 us: core_call(): pl.pallas_call(functools.partial(core_kernel, len(blocks), halves, bool(b...]
  transfers between devices with their start and end apart: 2 -> 16, of which waited for: 2 -> 4; matrix products, arithmetic and copies ran while one was open for 0% -> 0% of each run, Pallas kernels for 0% -> 17%
where the time goes in v2:
time: 64.6 us; the launch traced here: 64.2 us
  Pallas kernels  24 us (37%)
  starting transfers between devices  23.2 us (36%)
  waiting for transfers between devices  13.5 us (21%)
  local copies, waits for them, and re-layouts  3.36 us (5%)
    ppermute x15, starting transfers between devices, sent(): return lax.ppermute(array, 'vox', [(i, i ^ mask) for i in range(owners)])  21.6 us
    pallas_call x5, Pallas kernels, core_call(): pl.pallas_call(functools.partial(core_kernel, len(blocks), halves, bool(b...  12 us
    ppermute x15, waiting for transfers between devices, sent(): return lax.ppermute(array, 'vox', [(i, i ^ mask) for i in range(owners)])  7.87 us
    pallas_call x1, Pallas kernels, on_device(): pl.pallas_call(functools.partial(far_kernel, owners, capacity, echo_local...  5.85 us
    ppermute x1, waiting for transfers between devices, on_device(): got = lax.ppermute(give, 'echo', [(0, 1), (1, 0)])  5.63 us
    pallas_call x1, Pallas kernels, on_device(): pl.pallas_call(functools.partial(near_kernel, owners, capacity, echo_loca...  4.99 us
    unnamed x12, local copies, waits for them, and re-layouts  3.36 us
    ppermute x1, starting transfers between devices, on_device(): got = lax.ppermute(give, 'echo', [(0, 1), (1, 0)])  1.58 us
  transfers between devices with their start and end apart: 16, of which 4 were waited for; matrix products, arithmetic and copies ran while one was open for 0% of the time, Pallas kernels for 17%

profile of v2, /device:TPU:0, one launch (start us, length us, event | category | flops | bytes accessed | tf_op | source)
XLA Modules:
  0.0 64.2 jit_solution(7774532666642881778)
XLA Ops:
  0.0 0.0 copy-start.4
  0.0 0.7 %copy-done.4 = bf16[128,32]{0,1:T(8,128)(2,1)S(1)} copy-done((bf16[128,32]{0,1:T(8,128)(2,1)S(1)}, bf16[128,32]{0,1:T(8,128)(2,1)}, u32[]{:S(2)}) %copy-start.4) | copy-done | bytes 8216
  0.7 1.2 %copy-done = bf16[4096,128]{1,0:T(8,128)(2,1)S(1)} copy-done((bf16[4096,128]{1,0:T(8,128)(2,1)S(1)}, bf16[4096,128]{1,0:T(8,128)(2,1)}, u32[]{:S(2)}) %copy-start) | copy-done | bytes 1048600
  1.9 0.7 %copy-done.2 = s32[4096,1]{0,1:T(1,128)S(1)} copy-done((s32[4096,1]{0,1:T(1,128)S(1)}, s32[4096,1]{0,1:T(1,128)}, u32[]{:S(2)}) %copy-start.2) | copy-done | bytes 16408
  2.6 0.7 %copy-done.3 = s32[4096,1]{0,1:T(1,128)S(1)} copy-done((s32[4096,1]{0,1:T(1,128)S(1)}, s32[4096,1]{0,1:T(1,128)}, u32[]{:S(2)}) %copy-start.3) | copy-done | bytes 16408
  3.4 5.8 %far.1 = (bf16[32,4096]{1,0:T(8,128)(2,1)S(1)}, s32[8,1,512]{2,1,0:T(1,128)S(1)}, bf16[272,128]{1,0:T(8,128)(2,1)S(1)}, bf16[272,128]{1,0:T(8,128)(2,1)S(1)}, bf...) custom-call(s32[1]{0:T(128)} %bitcast.2.me_ref, ...), custom_call_target="tpu_custom_call" | custom-call | flops 2147483648 | bytes 2097152 | tf_op jit(solution)/shard_map/far/pallas_call | solution.py:293
  9.2 0.0 copy-start.1
  9.2 5.0 %near.1 = (bf16[272,128]{1,0:T(8,128)(2,1)S(1)}, bf16[272,128]{1,0:T(8,128)(2,1)S(1)}, bf16[272,128]{1,0:T(8,128)(2,1)S(1)}, bf16[272,128]{1,0:T(8,128)(2,1)S(1)...) custom-call(s32[1]{0:T(128)} %bitcast.2.me_ref, ...), custom_call_target="tpu_custom_call" | custom-call | flops 2147483648 | bytes 2097152 | tf_op jit(solution)/shard_map/near/pallas_call | solution.py:313
  14.2 0.5 collective-permute-start.8
  14.8 2.6 %collective-permute-start.9 = (bf16[272,128]{1,0:T(8,128)(2,1)S(1)}, bf16[272,128]{1,0:T(8,128)(2,1)S(1)}, u32[]{:S(2)}, u32[]{:S(2)}) collective-permute-start(bf16[272,128]{1,0:T(8,128)(2,1)S(1)} %get-tuple-element.41), channel_id=1, source_target_pairs={{0,4},{2,6},{4,0},{6,2},{8,12},{10,14},{12,8},{14,10},{16,20},{18,... | collective-permute-start | bytes 208904 | tf_op jit(solution)/shard_map/ppermute | solution.py:325
  17.3 0.1 collective-permute-start.10
  17.4 1.8 %collective-permute-start.11 = (bf16[272,128]{1,0:T(8,128)(2,1)S(1)}, bf16[272,128]{1,0:T(8,128)(2,1)S(1)}, u32[]{:S(2)}, u32[]{:S(2)}) collective-permute-start(bf16[272,128]{1,0:T(8,128)(2,1)S(1)} %get-tuple-element.43), channel_id=1, source_target_pairs={{0,8},{2,10},{4,12},{6,14},{8,0},{10,2},{12,4},{14,6},{16,24},{18,... | collective-permute-start | bytes 208904 | tf_op jit(solution)/shard_map/ppermute | solution.py:325
  19.2 0.0 collective-permute-start.12
  19.2 0.0 collective-permute-done.8.refs_1_
  19.2 2.6 %collective-permute-start.13 = (bf16[272,128]{1,0:T(8,128)(2,1)S(1)}, bf16[272,128]{1,0:T(8,128)(2,1)S(1)}, u32[]{:S(2)}, u32[]{:S(2)}) collective-permute-start(bf16[272,128]{1,0:T(8,128)(2,1)S(1)} %get-tuple-element.45), channel_id=1, source_target_pairs={{0,12},{2,14},{4,8},{6,10},{8,4},{10,6},{12,0},{14,2},{16,28},{18,... | collective-permute-start | bytes 208904 | tf_op jit(solution)/shard_map/ppermute | solution.py:325
  21.8 0.0 collective-permute-done.9.refs_2_
  21.8 0.3 collective-permute-start.14
  22.1 0.0 collective-permute-done.10.refs_3_
  22.1 3.4 %collective-permute-start = (bf16[272,128]{1,0:T(8,128)(2,1)S(1)}, bf16[272,128]{1,0:T(8,128)(2,1)S(1)}, u32[]{:S(2)}, u32[]{:S(2)}) collective-permute-start(bf16[272,128]{1,0:T(8,128)(2,1)S(1)} %get-tuple-element.29), channel_id=1, source_target_pairs={{0,26},{2,24},{4,30},{6,28},{8,18},{10,16},{12,22},{14,20},{16,10}... | collective-permute-start | bytes 208904 | tf_op jit(solution)/shard_map/ppermute | solution.py:325
  25.6 0.0 collective-permute-done.11.refs_4_
  25.6 0.0 collective-permute-start.4
  25.6 0.0 collective-permute-done.12.refs_5_
  25.6 3.9 %collective-permute-start.5 = (bf16[272,128]{1,0:T(8,128)(2,1)S(1)}, bf16[272,128]{1,0:T(8,128)(2,1)S(1)}, u32[]{:S(2)}, u32[]{:S(2)}) collective-permute-start(bf16[272,128]{1,0:T(8,128)(2,1)S(1)} %get-tuple-element.34), channel_id=1, source_target_pairs={{0,20},{2,22},{4,16},{6,18},{8,28},{10,30},{12,24},{14,26},{16,4},... | collective-permute-start | bytes 208904 | tf_op jit(solution)/shard_map/ppermute | solution.py:325
  29.4 0.0 collective-permute-done.13.refs_6_
  29.4 0.7 %collective-permute-start.6 = (bf16[272,128]{1,0:T(8,128)(2,1)S(1)}, bf16[272,128]{1,0:T(8,128)(2,1)S(1)}, u32[]{:S(2)}, u32[]{:S(2)}) collective-permute-start(bf16[272,128]{1,0:T(8,128)(2,1)S(1)} %get-tuple-element.35), channel_id=1, source_target_pairs={{0,24},{2,26},{4,28},{6,30},{8,16},{10,18},{12,20},{14,22},{16,8},... | collective-permute-start | bytes 208904 | tf_op jit(solution)/shard_map/ppermute | solution.py:325
  30.1 0.0 collective-permute-done.14.refs_7_
  30.1 3.1 %collective-permute-start.7 = (bf16[272,128]{1,0:T(8,128)(2,1)S(1)}, bf16[272,128]{1,0:T(8,128)(2,1)S(1)}, u32[]{:S(2)}, u32[]{:S(2)}) collective-permute-start(bf16[272,128]{1,0:T(8,128)(2,1)S(1)} %get-tuple-element.36), channel_id=1, source_target_pairs={{0,28},{2,30},{4,24},{6,26},{8,20},{10,22},{12,16},{14,18},{16,12}... | collective-permute-start | bytes 208904 | tf_op jit(solution)/shard_map/ppermute | solution.py:325
  33.2 0.0 copy-done.1
  33.2 0.0 copy-done.5
  33.2 5.3 %core.5 = (f32[512,256]{1,0:T(8,128)S(1)}, f32[512,256]{1,0:T(8,128)S(1)}) custom-call(s32[1]{0:T(128)} %bitcast.flip_ref, s32[256,128]{1,0:T(8,128)S(1)} %copy-done.1, bf16[32,128]{1,0:T(8,128)(2,1)S(1)} %bitcast.11, bf16[272,128]{1,0:T(8,128)(2,1)S(1)} %get-tuple-element.39.refs_0_, bf16[272,128]{1,0:T(8,128)(2,1)S(1)} %collective-permute-done.8.refs_1_, ...), custom_call_target="tpu_custom_call" | custom-call | flops 4294967296 | bytes 1605632 | tf_op jit(solution)/shard_map/core/pallas_call | solution.py:247
  38.6 0.0 collective-permute-done.4.refs_0_
  38.6 0.1 collective-permute-start.1
  38.7 1.5 %collective-permute-done.5.refs_1_ = bf16[272,128]{1,0:T(8,128)(2,1)S(1)} collective-permute-done((bf16[272,128]{1,0:T(8,128)(2,1)S(1)}, bf16[272,128]{1,0:T(8,128)(2,1)S(1)}, u32[]{:S(2)}, u32[]{:S(2)}) %collective-permute-start.5) | collective-permute-done | bytes 69664 | tf_op jit(solution)/shard_map/ppermute | solution.py:325
  40.1 0.0 collective-permute-start.2
  40.1 0.0 collective-permute-done.6.refs_2_
  40.1 2.6 %collective-permute-start.3 = (bf16[272,128]{1,0:T(8,128)(2,1)S(1)}, bf16[272,128]{1,0:T(8,128)(2,1)S(1)}, u32[]{:S(2)}, u32[]{:S(2)}) collective-permute-start(bf16[272,128]{1,0:T(8,128)(2,1)S(1)} %get-tuple-element.32), channel_id=1, source_target_pairs={{0,22},{2,20},{4,18},{6,16},{8,30},{10,28},{12,26},{14,24},{16,6},... | collective-permute-start | bytes 208904 | tf_op jit(solution)/shard_map/ppermute | solution.py:325
  42.7 0.0 collective-permute-done.7.refs_3_
  42.7 2.8 %core.6 = (f32[512,256]{1,0:T(8,128)S(1)}, f32[512,256]{1,0:T(8,128)S(1)}) custom-call(s32[1]{0:T(128)} %bitcast.flip_ref, s32[256,128]{1,0:T(8,128)S(1)} %copy-done.1, bf16[32,128]{1,0:T(8,128)(2,1)S(1)} %bitcast.12, bf16[272,128]{1,0:T(8,128)(2,1)S(1)} %collective-permute-done.4.refs_0_, ...), custom_call_target="tpu_custom_call", output_to_operand_aliasing={{0}: (7, {}), {1}: (8, {})} | custom-call | flops 2147483648 | bytes 1327104 | tf_op jit(solution)/shard_map/core/pallas_call | solution.py:247
  45.6 3.9 %collective-permute-done.2.refs_0_ = bf16[272,128]{1,0:T(8,128)(2,1)S(1)} collective-permute-done((bf16[272,128]{1,0:T(8,128)(2,1)S(1)}, bf16[272,128]{1,0:T(8,128)(2,1)S(1)}, u32[]{:S(2)}, u32[]{:S(2)}) %collective-permute-start.2) | collective-permute-done | bytes 69664 | tf_op jit(solution)/shard_map/ppermute | solution.py:325
  49.5 2.4 %collective-permute-done.3.refs_1_ = bf16[272,128]{1,0:T(8,128)(2,1)S(1)} collective-permute-done((bf16[272,128]{1,0:T(8,128)(2,1)S(1)}, bf16[272,128]{1,0:T(8,128)(2,1)S(1)}, u32[]{:S(2)}, u32[]{:S(2)}) %collective-permute-start.3) | collective-permute-done | bytes 69664 | tf_op jit(solution)/shard_map/ppermute | solution.py:325
  51.9 1.6 %core.7 = (f32[512,256]{1,0:T(8,128)S(1)}, f32[512,256]{1,0:T(8,128)S(1)}) custom-call(s32[1]{0:T(128)} %bitcast.flip_ref, s32[256,128]{1,0:T(8,128)S(1)} %copy-done.1, bf16[32,128]{1,0:T(8,128)(2,1)S(1)} %bitcast.13, bf16[272,128]{1,0:T(8,128)(2,1)S(1)} %collective-permute-done.2.refs_0_, ...), custom_call_target="tpu_custom_call", output_to_operand_aliasing={{0}: (5, {}), {1}: (6, {})} | custom-call | flops 1073741824 | bytes 1187840 | tf_op jit(solution)/shard_map/core/pallas_call | solution.py:247
  53.5 0.0 collective-permute-done.refs_0_
  53.6 0.0 collective-permute-done.1.refs_1_
  53.6 1.0 %core.9 = bf16[512,256]{1,0:T(8,128)(2,1)S(1)} custom-call(s32[1]{0:T(128)} %bitcast.flip_ref, s32[256,128]{1,0:T(8,128)S(1)} %copy-done.1, bf16[32,128]{1,0:T(8,128)(2,1)S(1)} %bitcast.14, bf16[272,128]{1,0:T(8,128)(2,1)S(1)} %collective-permute-done.refs_0_, bf16[272,128]{1,0:T(8,128)(2,1)S(1)} %collective-permute-done.1.refs_1_, ...), custom_call_target="tpu_custom_call" | custom-call | flops 536870912 | bytes 663552 | tf_op jit(solution)/shard_map/core/pallas_call | solution.py:247
  54.6 1.6 %collective-permute-start.15 = (bf16[512,256]{1,0:T(8,128)(2,1)S(1)}, bf16[512,256]{1,0:T(8,128)(2,1)S(1)}, u32[]{:S(2)}, u32[]{:S(2)}) collective-permute-start(bf16[512,256]{1,0:T(8,128)(2,1)S(1)} %core.9), channel_id=1, source_target_pairs={{0,1},{1,0},{2,3},{3,2},{4,5},{5,4},{6,7},{7,6},{8,9},{9,8},{10,11... | collective-permute-start | bytes 786440 | tf_op jit(solution)/shard_map/ppermute | solution.py:347
  56.2 1.2 %core.8.keep_ref = f32[512,256]{1,0:T(8,128)S(1)} custom-call(s32[1]{0:T(128)} %bitcast.flip_ref, s32[256,128]{1,0:T(8,128)S(1)} %copy-done.1, bf16[32,128]{1,0:T(8,128)(2,1)S(1)} %bitcast.15, bf16[272,128]{1,0:T(8,128)(2,1)S(1)} %collective-permute-done.refs_0_, ...), custom_call_target="tpu_custom_call", output_to_operand_aliasing={{}: (5, {})} | custom-call | flops 536870912 | bytes 663552 | tf_op jit(solution)/shard_map/core/pallas_call | solution.py:247
  57.4 5.6 %collective-permute-done.15.got_ref = bf16[512,256]{1,0:T(8,128)(2,1)S(1)} collective-permute-done((bf16[512,256]{1,0:T(8,128)(2,1)S(1)}, bf16[512,256]{1,0:T(8,128)(2,1)S(1)}, u32[]{:S(2)}, u32[]{:S(2)}) %collective-permute-start.15) | collective-permute-done | bytes 262176 | tf_op jit(solution)/shard_map/ppermute | solution.py:347
  63.0 1.2 %finish.1 = bf16[128,1024]{1,0:T(8,128)(2,1)} custom-call(f32[512,256]{1,0:T(8,128)S(1)} %core.8.keep_ref, bf16[512,256]{1,0:T(8,128)(2,1)S(1)} %collective-permute-done.15.got_ref), custom_call_target="tpu_custom_call" | custom-call | tf_op jit(solution)/shard_map/finish/pallas_call | solution.py:349
  (4 shorter events, 0.0 us)
Async XLA Ops:
  0.0 0.7 %copy-start.4 = (bf16[128,32]{0,1:T(8,128)(2,1)S(1)}, bf16[128,32]{0,1:T(8,128)(2,1)}, u32[]{:S(2)}) copy-start(bf16[128,32]{0,1:T(8,128)(2,1)} %param.10) | copy-start | bytes 24580
  0.7 1.2 %copy-start = (bf16[4096,128]{1,0:T(8,128)(2,1)S(1)}, bf16[4096,128]{1,0:T(8,128)(2,1)}, u32[]{:S(2)}) copy-start(bf16[4096,128]{1,0:T(8,128)(2,1)} %acquired_hbm.1) | copy-start | bytes 3145732
  1.9 0.7 %copy-start.2 = (s32[4096,1]{0,1:T(1,128)S(1)}, s32[4096,1]{0,1:T(1,128)}, u32[]{:S(2)}) copy-start(s32[4096,1]{0,1:T(1,128)} %param.7) | copy-start | bytes 49156
  2.6 0.7 %copy-start.3 = (s32[4096,1]{0,1:T(1,128)S(1)}, s32[4096,1]{0,1:T(1,128)}, u32[]{:S(2)}) copy-start(s32[4096,1]{0,1:T(1,128)} %param.8) | copy-start | bytes 49156
  9.2 24.0 %copy-start.1 = (s32[256,128]{1,0:T(8,128)S(1)}, s32[256,128]{1,0:T(8,128)}, u32[]{:S(2)}) copy-start(s32[256,128]{1,0:T(8,128)} %sampled_ref.9) | copy-start | bytes 393220
  14.2 5.0 %collective-permute-start.8 = (bf16[272,128]{1,0:T(8,128)(2,1)S(1)}, bf16[272,128]{1,0:T(8,128)(2,1)S(1)}, u32[]{:S(2)}, u32[]{:S(2)}) collective-permute-start(bf16[272,128]{1,0:T(8,128)(2,1)S(1)} %get-tuple-element.40), channel_id=1, source_target_pairs={{0,2},{2,0},{4,6},{6,4},{8,10},{10,8},{12,14},{14,12},{16,18},{18,... | collective-permute-start | bytes 208904 | tf_op jit(solution)/shard_map/ppermute | solution.py:325
  14.8 7.1 %collective-permute-start.9 = (bf16[272,128]{1,0:T(8,128)(2,1)S(1)}, bf16[272,128]{1,0:T(8,128)(2,1)S(1)}, u32[]{:S(2)}, u32[]{:S(2)}) collective-permute-start(bf16[272,128]{1,0:T(8,128)(2,1)S(1)} %get-tuple-element.41), channel_id=1, source_target_pairs={{0,4},{2,6},{4,0},{6,2},{8,12},{10,14},{12,8},{14,10},{16,20},{18,... | collective-permute-start | bytes 208904 | tf_op jit(solution)/shard_map/ppermute | solution.py:325
  17.3 4.8 %collective-permute-start.10 = (bf16[272,128]{1,0:T(8,128)(2,1)S(1)}, bf16[272,128]{1,0:T(8,128)(2,1)S(1)}, u32[]{:S(2)}, u32[]{:S(2)}) collective-permute-start(bf16[272,128]{1,0:T(8,128)(2,1)S(1)} %get-tuple-element.42), channel_id=1, source_target_pairs={{0,6},{2,4},{4,2},{6,0},{8,14},{10,12},{12,10},{14,8},{16,22},{18,... | collective-permute-start | bytes 208904 | tf_op jit(solution)/shard_map/ppermute | solution.py:325
  17.4 8.2 %collective-permute-start.11 = (bf16[272,128]{1,0:T(8,128)(2,1)S(1)}, bf16[272,128]{1,0:T(8,128)(2,1)S(1)}, u32[]{:S(2)}, u32[]{:S(2)}) collective-permute-start(bf16[272,128]{1,0:T(8,128)(2,1)S(1)} %get-tuple-element.43), channel_id=1, source_target_pairs={{0,8},{2,10},{4,12},{6,14},{8,0},{10,2},{12,4},{14,6},{16,24},{18,... | collective-permute-start | bytes 208904 | tf_op jit(solution)/shard_map/ppermute | solution.py:325
  19.2 6.4 %collective-permute-start.12 = (bf16[272,128]{1,0:T(8,128)(2,1)S(1)}, bf16[272,128]{1,0:T(8,128)(2,1)S(1)}, u32[]{:S(2)}, u32[]{:S(2)}) collective-permute-start(bf16[272,128]{1,0:T(8,128)(2,1)S(1)} %get-tuple-element.44), channel_id=1, source_target_pairs={{0,10},{2,8},{4,14},{6,12},{8,2},{10,0},{12,6},{14,4},{16,26},{18,... | collective-permute-start | bytes 208904 | tf_op jit(solution)/shard_map/ppermute | solution.py:325
  19.2 10.2 %collective-permute-start.13 = (bf16[272,128]{1,0:T(8,128)(2,1)S(1)}, bf16[272,128]{1,0:T(8,128)(2,1)S(1)}, u32[]{:S(2)}, u32[]{:S(2)}) collective-permute-start(bf16[272,128]{1,0:T(8,128)(2,1)S(1)} %get-tuple-element.45), channel_id=1, source_target_pairs={{0,12},{2,14},{4,8},{6,10},{8,4},{10,6},{12,0},{14,2},{16,28},{18,... | collective-permute-start | bytes 208904 | tf_op jit(solution)/shard_map/ppermute | solution.py:325
  21.8 8.3 %collective-permute-start.14 = (bf16[272,128]{1,0:T(8,128)(2,1)S(1)}, bf16[272,128]{1,0:T(8,128)(2,1)S(1)}, u32[]{:S(2)}, u32[]{:S(2)}) collective-permute-start(bf16[272,128]{1,0:T(8,128)(2,1)S(1)} %get-tuple-element.46), channel_id=1, source_target_pairs={{0,14},{2,12},{4,10},{6,8},{8,6},{10,4},{12,2},{14,0},{16,30},{18,... | collective-permute-start | bytes 208904 | tf_op jit(solution)/shard_map/ppermute | solution.py:325
  22.1 11.1 %copy-start.5 = (bf16[128,32]{0,1:T(8,128)(2,1)S(1)}, bf16[128,32]{0,1:T(8,128)(2,1)}, u32[]{:S(2)}) copy-start(bf16[128,32]{0,1:T(8,128)(2,1)} %param.11) | copy-start | bytes 24580
  22.1 31.4 %collective-permute-start = (bf16[272,128]{1,0:T(8,128)(2,1)S(1)}, bf16[272,128]{1,0:T(8,128)(2,1)S(1)}, u32[]{:S(2)}, u32[]{:S(2)}) collective-permute-start(bf16[272,128]{1,0:T(8,128)(2,1)S(1)} %get-tuple-element.29), channel_id=1, source_target_pairs={{0,26},{2,24},{4,30},{6,28},{8,18},{10,16},{12,22},{14,20},{16,10}... | collective-permute-start | bytes 208904 | tf_op jit(solution)/shard_map/ppermute | solution.py:325
  25.6 13.0 %collective-permute-start.4 = (bf16[272,128]{1,0:T(8,128)(2,1)S(1)}, bf16[272,128]{1,0:T(8,128)(2,1)S(1)}, u32[]{:S(2)}, u32[]{:S(2)}) collective-permute-start(bf16[272,128]{1,0:T(8,128)(2,1)S(1)} %get-tuple-element.33), channel_id=1, source_target_pairs={{0,16},{2,18},{4,20},{6,22},{8,24},{10,26},{12,28},{14,30},{16,0},... | collective-permute-start | bytes 208904 | tf_op jit(solution)/shard_map/ppermute | solution.py:325
  25.6 14.6 %collective-permute-start.5 = (bf16[272,128]{1,0:T(8,128)(2,1)S(1)}, bf16[272,128]{1,0:T(8,128)(2,1)S(1)}, u32[]{:S(2)}, u32[]{:S(2)}) collective-permute-start(bf16[272,128]{1,0:T(8,128)(2,1)S(1)} %get-tuple-element.34), channel_id=1, source_target_pairs={{0,20},{2,22},{4,16},{6,18},{8,28},{10,30},{12,24},{14,26},{16,4},... | collective-permute-start | bytes 208904 | tf_op jit(solution)/shard_map/ppermute | solution.py:325
  29.4 10.7 %collective-permute-start.6 = (bf16[272,128]{1,0:T(8,128)(2,1)S(1)}, bf16[272,128]{1,0:T(8,128)(2,1)S(1)}, u32[]{:S(2)}, u32[]{:S(2)}) collective-permute-start(bf16[272,128]{1,0:T(8,128)(2,1)S(1)} %get-tuple-element.35), channel_id=1, source_target_pairs={{0,24},{2,26},{4,28},{6,30},{8,16},{10,18},{12,20},{14,22},{16,8},... | collective-permute-start | bytes 208904 | tf_op jit(solution)/shard_map/ppermute | solution.py:325
  30.1 12.6 %collective-permute-start.7 = (bf16[272,128]{1,0:T(8,128)(2,1)S(1)}, bf16[272,128]{1,0:T(8,128)(2,1)S(1)}, u32[]{:S(2)}, u32[]{:S(2)}) collective-permute-start(bf16[272,128]{1,0:T(8,128)(2,1)S(1)} %get-tuple-element.36), channel_id=1, source_target_pairs={{0,28},{2,30},{4,24},{6,26},{8,20},{10,22},{12,16},{14,18},{16,12}... | collective-permute-start | bytes 208904 | tf_op jit(solution)/shard_map/ppermute | solution.py:325
  38.6 15.0 %collective-permute-start.1 = (bf16[272,128]{1,0:T(8,128)(2,1)S(1)}, bf16[272,128]{1,0:T(8,128)(2,1)S(1)}, u32[]{:S(2)}, u32[]{:S(2)}) collective-permute-start(bf16[272,128]{1,0:T(8,128)(2,1)S(1)} %get-tuple-element.30), channel_id=1, source_target_pairs={{0,30},{2,28},{4,26},{6,24},{8,22},{10,20},{12,18},{14,16},{16,14}... | collective-permute-start | bytes 208904 | tf_op jit(solution)/shard_map/ppermute | solution.py:325
  40.1 9.4 %collective-permute-start.2 = (bf16[272,128]{1,0:T(8,128)(2,1)S(1)}, bf16[272,128]{1,0:T(8,128)(2,1)S(1)}, u32[]{:S(2)}, u32[]{:S(2)}) collective-permute-start(bf16[272,128]{1,0:T(8,128)(2,1)S(1)} %get-tuple-element.31), channel_id=1, source_target_pairs={{0,18},{2,16},{4,22},{6,20},{8,26},{10,24},{12,30},{14,28},{16,2},... | collective-permute-start | bytes 208904 | tf_op jit(solution)/shard_map/ppermute | solution.py:325
  40.1 11.8 %collective-permute-start.3 = (bf16[272,128]{1,0:T(8,128)(2,1)S(1)}, bf16[272,128]{1,0:T(8,128)(2,1)S(1)}, u32[]{:S(2)}, u32[]{:S(2)}) collective-permute-start(bf16[272,128]{1,0:T(8,128)(2,1)S(1)} %get-tuple-element.32), channel_id=1, source_target_pairs={{0,22},{2,20},{4,18},{6,16},{8,30},{10,28},{12,26},{14,24},{16,6},... | collective-permute-start | bytes 208904 | tf_op jit(solution)/shard_map/ppermute | solution.py:325
  54.6 8.4 %collective-permute-start.15 = (bf16[512,256]{1,0:T(8,128)(2,1)S(1)}, bf16[512,256]{1,0:T(8,128)(2,1)S(1)}, u32[]{:S(2)}, u32[]{:S(2)}) collective-permute-start(bf16[512,256]{1,0:T(8,128)(2,1)S(1)} %core.9), channel_id=1, source_target_pairs={{0,1},{1,0},{2,3},{3,2},{4,5},{5,4},{6,7},{7,6},{8,9},{9,8},{10,11... | collective-permute-start | bytes 786440 | tf_op jit(solution)/shard_map/ppermute | solution.py:347

commit v3 on v2

--- a/solution.py
+++ b/solution.py
@@ -9,6 +9,7 @@
 
 LANES = 128
 CHUNK = 512
+STEP = 1024
 FINE = 16
 BF16 = jnp.bfloat16
 F32 = jnp.float32
@@ -50,43 +51,43 @@
 
 def put_rows(
     first, capacity, echo_local, me, reduced_ref, owner_ref, slot_ref, place_ref,
-    out_refs, feature_ref, id_ref,
+    out_refs, spread_ref, hot_ref, ids_ref,
 ):
     rank, rows = reduced_ref.shape
     count = len(out_refs)
     groups = capacity // LANES
-    lane_range = lax.broadcasted_iota(I32, (LANES, CHUNK), 0)
-    group_range = lax.broadcasted_iota(I32, (8, CHUNK), 0)
-
-    def step(j, _):
-        at = pl.multiple_of(j * CHUNK, CHUNK)
-        reduced = reduced_ref[:, pl.ds(at, CHUNK)]
-        relative = owner_ref[:, pl.ds(at, CHUNK)] ^ me
-        slot = slot_ref[:, pl.ds(at, CHUNK)]
-        place = place_ref[j]
+    lane_range = lax.broadcasted_iota(I32, (LANES, STEP), 0).astype(F32).astype(BF16)
+    group_range = lax.broadcasted_iota(I32, (8, STEP), 0)
+
+    def level(row, height):
+        return jnp.broadcast_to(row.astype(F32), (height, STEP)).astype(BF16)
+
+    for j in range(rows // STEP):
+        at = slice(j * STEP, (j + 1) * STEP)
+        reduced = reduced_ref[:, at]
+        relative = owner_ref[:, at] ^ me
+        slot = slot_ref[:, at]
+        place = jnp.concatenate(
+            [place_ref[j * (STEP // CHUNK) + i] for i in range(STEP // CHUNK)], axis=1
+        )
         group = place // LANES
-        lane_hot = (lane_range == place % LANES).astype(F32).astype(BF16)
-        group_b = jnp.broadcast_to(group.astype(F32), (LANES, CHUNK)).astype(BF16)
-        place_hot = jnp.concatenate(
-            [
-                jnp.where(group_b == BF16(g), lane_hot, BF16(0))
-                for g in range(groups)
-            ],
-            axis=0,
-        )
+        lane = level(place % LANES, LANES)
+        lane_hot = jnp.where(lane_range == lane, BF16(1), BF16(0))
+        group_b = level(group, LANES)
+        for g in range(groups):
+            hot_ref[g * LANES : (g + 1) * LANES, at] = jnp.where(
+                group_b == BF16(g), lane_hot, BF16(0)
+            )
         here = group_range == group
         voxel = jnp.where(here, (slot // echo_local).astype(F32), 0.0)
         echo = jnp.where(here, (slot % echo_local).astype(F32), 0.0)
         ids = jnp.concatenate([voxel, echo], axis=0).astype(BF16)
-        owner_b = jnp.broadcast_to(relative.astype(F32), (rank, CHUNK)).astype(BF16)
-        owner_c = owner_b[:16]
-        spread = jnp.concatenate(
-            [
-                jnp.where(owner_b == BF16(first + o), reduced, BF16(0))
-                for o in range(count)
-            ],
-            axis=0,
-        )
+        owner_b = level(relative, rank)
+        owner_c = level(relative, 16)
+        for o in range(count):
+            spread_ref[o * rank : (o + 1) * rank, at] = jnp.where(
+                owner_b == BF16(first + o), reduced, BF16(0)
+            )
         spread_ids = jnp.concatenate(
             [
                 jnp.where(owner_c == BF16(first + o), ids, BF16(0))
@@ -94,40 +95,35 @@
             ],
             axis=0,
         )
-        feature = nt_dot(spread, place_hot)
-        id_sum = nt_dot(spread_ids, lane_hot)
-
-        @pl.when(j == 0)
-        def _():
-            feature_ref[...] = feature
-            id_ref[...] = id_sum
-
-        @pl.when(j > 0)
-        def _():
-            feature_ref[...] += feature
-            id_ref[...] += id_sum
-
-        return 0
-
-    lax.fori_loop(0, rows // CHUNK, step, 0)
+        part = nt_dot(spread_ids, lane_hot)
+        ids_ref[...] = part if j == 0 else ids_ref[...] + part
     for o in range(count):
-        for g in range(groups):
-            out_refs[o][g * rank : (g + 1) * rank, :] = feature_ref[
-                o * rank : (o + 1) * rank, g * LANES : (g + 1) * LANES
-            ].astype(BF16)
-        out_refs[o][groups * rank :, :] = id_ref[o * 16 : (o + 1) * 16, :].astype(BF16)
+        out_refs[o][groups * rank :, :] = ids_ref[o * 16 : (o + 1) * 16, :].astype(BF16)
+    wide = 2 * LANES
+    for g in range(0, groups, 2):
+        made = nt_dot(spread_ref[...], hot_ref[g * LANES : g * LANES + wide, :]).astype(BF16)
+        for o in range(count):
+            for i in range(2):
+                out_refs[o][(g + i) * rank : (g + i + 1) * rank, :] = made[
+                    o * rank : (o + 1) * rank, i * LANES : (i + 1) * LANES
+                ]
 
 
 def far_kernel(
-    owners, capacity, echo_local, me_ref, acquired_hbm, owner_hbm, slot_hbm, left_ref,
-    reduced_ref, place_ref, *refs,
+    owners, capacity, echo_local, me_ref, acquired_hbm, owner_hbm, slot_hbm, left_hbm,
+    reduced_ref, place_ref, owner_ref, slot_ref, *refs,
 ):
     outs = refs[: owners // 2]
-    acquired_ref, owner_ref, slot_ref, feature_ref, id_ref, sems = refs[owners // 2 :]
+    acquired_ref, left_ref, spread_ref, hot_ref, ids_ref, sems = refs[owners // 2 :]
     copies = [
         pltpu.make_async_copy(a, b, sems.at[i])
         for i, (a, b) in enumerate(
-            [(owner_hbm, owner_ref), (slot_hbm, slot_ref), (acquired_hbm, acquired_ref)]
+            [
+                (owner_hbm, owner_ref),
+                (slot_hbm, slot_ref),
+                (acquired_hbm, acquired_ref),
+                (left_hbm, left_ref),
+            ]
         )
     ]
     for copy in copies:
@@ -135,12 +131,12 @@
     copies[0].wait()
     me = me_ref[0]
     place_rows(owners, me, owner_ref, place_ref)
-    copies[1].wait()
-    copies[2].wait()
+    for copy in copies[1:]:
+        copy.wait()
     reduced_ref[...] = nt_dot(left_ref[...], acquired_ref[...]).astype(BF16)
     put_rows(
         owners // 2, capacity, echo_local, me, reduced_ref, owner_ref, slot_ref, place_ref,
-        outs, feature_ref, id_ref,
+        outs, spread_ref, hot_ref, ids_ref,
     )
 
 
@@ -233,7 +229,7 @@
 
 VMEM = pl.BlockSpec(memory_space=pltpu.VMEM)
 SMEM = pl.BlockSpec(memory_space=pltpu.SMEM)
-ANY = pl.BlockSpec(memory_space=pl.ANY)
+HBM = pl.BlockSpec(memory_space=pltpu.HBM)
 PARAMS = pltpu.CompilerParams(vmem_limit_bytes=40 * 2**20)
 
 
@@ -282,7 +278,8 @@
     left, right = left_panel.T, right_panel.T
     block = jax.ShapeDtypeStruct((depth, LANES), BF16)
     sums = [
-        pltpu.VMEM((half * rank, capacity), F32),
+        pltpu.VMEM((half * rank, rows), BF16),
+        pltpu.VMEM((capacity, rows), BF16),
         pltpu.VMEM((half * 16, LANES), F32),
     ]
     cost = pl.CostEstimate(
@@ -290,26 +287,27 @@
         bytes_accessed=4 * rows * 128,
         transcendentals=0,
     )
-    reduced, place, *far = pl.pallas_call(
+    reduced, place, owner, slot, *far = pl.pallas_call(
         functools.partial(far_kernel, owners, capacity, echo_local),
         out_shape=[
             jax.ShapeDtypeStruct((rank, rows), BF16),
             jax.ShapeDtypeStruct((rows // CHUNK, 1, CHUNK), I32),
+            jax.ShapeDtypeStruct(owner.shape, I32),
+            jax.ShapeDtypeStruct(slot.shape, I32),
         ]
         + [block] * half,
-        in_specs=[SMEM, ANY, ANY, ANY, VMEM],
-        out_specs=[VMEM] * (2 + half),
+        in_specs=[SMEM, HBM, HBM, HBM, HBM],
+        out_specs=[VMEM] * (4 + half),
         scratch_shapes=[
             pltpu.VMEM(acquired.shape, BF16),
-            pltpu.VMEM(owner.shape, I32),
-            pltpu.VMEM(slot.shape, I32),
+            pltpu.VMEM(left.shape, BF16),
             *sums,
-            pltpu.SemaphoreType.DMA((3,)),
+            pltpu.SemaphoreType.DMA((4,)),
         ],
         compiler_params=PARAMS,
         cost_estimate=cost,
         name="far",
-    )(me, acquired, owner, slot, left)
+    )(me, *[pltpu.with_memory_space_constraint(x, pltpu.HBM) for x in (acquired, owner, slot, left)])
     near = pl.pallas_call(
         functools.partial(near_kernel, owners, capacity, echo_local),
         out_shape=[block] * half,

time: 64.6 us -> 57.2 us (0.89)
  Pallas kernels: 24 us -> 20.3 us
  local copies, waits for them, and re-layouts: 3.36 us -> 0.01 us
    unnamed x12 -> x4, local copies, waits for them, and re-layouts: 3.36 us -> 0.01 us
    pallas_call x1, Pallas kernels: 4.99 us -> 2.64 us  [on_device(): pl.pallas_call(functools.partial(near_kernel, owners, capacity, echo_loca...]
    pallas_call x1, Pallas kernels: 5.85 us -> 4.29 us  [on_device(): pl.pallas_call(functools.partial(far_kernel, owners, capacity, echo_local...]
  transfers between devices with their start and end apart: 16 -> 16, of which waited for: 4 -> 4; matrix products, arithmetic and copies ran while one was open for 0% -> 0% of each run, Pallas kernels for 17% -> 20%
where the time goes in v3:
time: 57.2 us; the launch traced here: 56.9 us
  starting transfers between devices  23.3 us (41%)
  Pallas kernels  20.3 us (35%)
  waiting for transfers between devices  13.2 us (23%)
    ppermute x15, starting transfers between devices, sent(): return lax.ppermute(array, 'vox', [(i, i ^ mask) for i in range(owners)])  21.7 us
    pallas_call x5, Pallas kernels, core_call(): pl.pallas_call(functools.partial(core_kernel, len(blocks), halves, bool(b...  12.2 us
    ppermute x15, waiting for transfers between devices, sent(): return lax.ppermute(array, 'vox', [(i, i ^ mask) for i in range(owners)])  7.63 us
    ppermute x1, waiting for transfers between devices, on_device(): got = lax.ppermute(give, 'echo', [(0, 1), (1, 0)])  5.61 us
    pallas_call x1, Pallas kernels, on_device(): pl.pallas_call(functools.partial(far_kernel, owners, capacity, echo_local...  4.29 us
    pallas_call x1, Pallas kernels, on_device(): pl.pallas_call(functools.partial(near_kernel, owners, capacity, echo_loca...  2.64 us
    ppermute x1, starting transfers between devices, on_device(): got = lax.ppermute(give, 'echo', [(0, 1), (1, 0)])  1.59 us
    pallas_call x1, Pallas kernels, on_device(): pl.pallas_call(functools.partial(finish_kernel, rank), out_shape=jax.Shap...  1.2 us
  transfers between devices with their start and end apart: 16, of which 4 were waited for; matrix products, arithmetic and copies ran while one was open for 0% of the time, Pallas kernels for 20%

profile of v3, /device:TPU:0, one launch (start us, length us, event | category | flops | bytes accessed | tf_op | source)
XLA Modules:
  0.0 56.9 jit_solution(1043973201258468817)
XLA Ops:
  0.0 4.3 %far.1 = (bf16[32,4096]{1,0:T(8,128)(2,1)S(1)}, s32[8,1,512]{2,1,0:T(1,128)S(1)}, s32[1,4096]{1,0:T(1,128)S(1)}, s32[1,4096]{1,0:T(1,128)S(1)}, bf16[272,128]{1,...) custom-call(s32[1]{0:T(128)} %bitcast.2.me_ref, ...), custom_call_target="tpu_custom_call" | custom-call | flops 2147483648 | bytes 2097152 | tf_op jit(solution)/shard_map/far/pallas_call | solution.py:290
  4.3 0.0 copy-start
  4.3 2.6 %near.1 = (bf16[272,128]{1,0:T(8,128)(2,1)S(1)}, bf16[272,128]{1,0:T(8,128)(2,1)S(1)}, bf16[272,128]{1,0:T(8,128)(2,1)S(1)}, bf16[272,128]{1,0:T(8,128)(2,1)S(1)...) custom-call(s32[1]{0:T(128)} %bitcast.2.me_ref, ...), custom_call_target="tpu_custom_call" | custom-call | flops 2147483648 | bytes 2097152 | tf_op jit(solution)/shard_map/near/pallas_call | solution.py:311
  7.0 0.5 collective-permute-start.8
  7.5 2.6 %collective-permute-start.9 = (bf16[272,128]{1,0:T(8,128)(2,1)S(1)}, bf16[272,128]{1,0:T(8,128)(2,1)S(1)}, u32[]{:S(2)}, u32[]{:S(2)}) collective-permute-start(bf16[272,128]{1,0:T(8,128)(2,1)S(1)} %get-tuple-element.45), channel_id=1, source_target_pairs={{0,4},{2,6},{4,0},{6,2},{8,12},{10,14},{12,8},{14,10},{16,20},{18,... | collective-permute-start | bytes 208904 | tf_op jit(solution)/shard_map/ppermute | solution.py:323
  10.0 0.1 collective-permute-start.10
  10.1 1.8 %collective-permute-start.11 = (bf16[272,128]{1,0:T(8,128)(2,1)S(1)}, bf16[272,128]{1,0:T(8,128)(2,1)S(1)}, u32[]{:S(2)}, u32[]{:S(2)}) collective-permute-start(bf16[272,128]{1,0:T(8,128)(2,1)S(1)} %get-tuple-element.47), channel_id=1, source_target_pairs={{0,8},{2,10},{4,12},{6,14},{8,0},{10,2},{12,4},{14,6},{16,24},{18,... | collective-permute-start | bytes 208904 | tf_op jit(solution)/shard_map/ppermute | solution.py:323
  11.9 0.0 collective-permute-start.12
  11.9 0.0 collective-permute-done.8.refs_1_
  11.9 2.6 %collective-permute-start.13 = (bf16[272,128]{1,0:T(8,128)(2,1)S(1)}, bf16[272,128]{1,0:T(8,128)(2,1)S(1)}, u32[]{:S(2)}, u32[]{:S(2)}) collective-permute-start(bf16[272,128]{1,0:T(8,128)(2,1)S(1)} %get-tuple-element.49), channel_id=1, source_target_pairs={{0,12},{2,14},{4,8},{6,10},{8,4},{10,6},{12,0},{14,2},{16,28},{18,... | collective-permute-start | bytes 208904 | tf_op jit(solution)/shard_map/ppermute | solution.py:323
  14.5 0.0 collective-permute-done.9.refs_2_
  14.6 0.3 collective-permute-start.14
  14.8 0.0 copy-start.1
  14.9 0.0 collective-permute-done.10.refs_3_
  14.9 3.4 %collective-permute-start = (bf16[272,128]{1,0:T(8,128)(2,1)S(1)}, bf16[272,128]{1,0:T(8,128)(2,1)S(1)}, u32[]{:S(2)}, u32[]{:S(2)}) collective-permute-start(bf16[272,128]{1,0:T(8,128)(2,1)S(1)} %get-tuple-element.31), channel_id=1, source_target_pairs={{0,26},{2,24},{4,30},{6,28},{8,18},{10,16},{12,22},{14,20},{16,10}... | collective-permute-start | bytes 208904 | tf_op jit(solution)/shard_map/ppermute | solution.py:323
  18.3 0.0 collective-permute-done.11.refs_4_
  18.3 0.0 collective-permute-start.4
  18.3 0.0 collective-permute-done.12.refs_5_
  18.3 3.8 %collective-permute-start.5 = (bf16[272,128]{1,0:T(8,128)(2,1)S(1)}, bf16[272,128]{1,0:T(8,128)(2,1)S(1)}, u32[]{:S(2)}, u32[]{:S(2)}) collective-permute-start(bf16[272,128]{1,0:T(8,128)(2,1)S(1)} %get-tuple-element.36), channel_id=1, source_target_pairs={{0,20},{2,22},{4,16},{6,18},{8,28},{10,30},{12,24},{14,26},{16,4},... | collective-permute-start | bytes 208904 | tf_op jit(solution)/shard_map/ppermute | solution.py:323
  22.2 0.0 collective-permute-done.13.refs_6_
  22.2 0.7 %collective-permute-start.6 = (bf16[272,128]{1,0:T(8,128)(2,1)S(1)}, bf16[272,128]{1,0:T(8,128)(2,1)S(1)}, u32[]{:S(2)}, u32[]{:S(2)}) collective-permute-start(bf16[272,128]{1,0:T(8,128)(2,1)S(1)} %get-tuple-element.37), channel_id=1, source_target_pairs={{0,24},{2,26},{4,28},{6,30},{8,16},{10,18},{12,20},{14,22},{16,8},... | collective-permute-start | bytes 208904 | tf_op jit(solution)/shard_map/ppermute | solution.py:323
  22.9 0.0 collective-permute-done.14.refs_7_
  22.9 3.1 %collective-permute-start.7 = (bf16[272,128]{1,0:T(8,128)(2,1)S(1)}, bf16[272,128]{1,0:T(8,128)(2,1)S(1)}, u32[]{:S(2)}, u32[]{:S(2)}) collective-permute-start(bf16[272,128]{1,0:T(8,128)(2,1)S(1)} %get-tuple-element.38), channel_id=1, source_target_pairs={{0,28},{2,30},{4,24},{6,26},{8,20},{10,22},{12,16},{14,18},{16,12}... | collective-permute-start | bytes 208904 | tf_op jit(solution)/shard_map/ppermute | solution.py:323
  26.0 0.0 copy-done
  26.0 0.0 copy-done.1
  26.0 5.3 %core.5 = (f32[512,256]{1,0:T(8,128)S(1)}, f32[512,256]{1,0:T(8,128)S(1)}) custom-call(s32[1]{0:T(128)} %bitcast.flip_ref, s32[256,128]{1,0:T(8,128)S(1)} %copy-done, bf16[32,128]{1,0:T(8,128)(2,1)S(1)} %bitcast.6, bf16[272,128]{1,0:T(8,128)(2,1)S(1)} %get-tuple-element.43.refs_0_, bf16[272,128]{1,0:T(8,128)(2,1)S(1)} %collective-permute-done.8.refs_1_, ...), custom_call_target="tpu_custom_call" | custom-call | flops 4294967296 | bytes 1605632 | tf_op jit(solution)/shard_map/core/pallas_call | solution.py:243
  31.3 0.0 collective-permute-done.4.refs_0_
  31.3 0.1 collective-permute-start.1
  31.4 1.5 %collective-permute-done.5.refs_1_ = bf16[272,128]{1,0:T(8,128)(2,1)S(1)} collective-permute-done((bf16[272,128]{1,0:T(8,128)(2,1)S(1)}, bf16[272,128]{1,0:T(8,128)(2,1)S(1)}, u32[]{:S(2)}, u32[]{:S(2)}) %collective-permute-start.5) | collective-permute-done | bytes 69664 | tf_op jit(solution)/shard_map/ppermute | solution.py:323
  32.9 0.0 collective-permute-start.2
  32.9 0.0 collective-permute-done.6.refs_2_
  32.9 2.6 %collective-permute-start.3 = (bf16[272,128]{1,0:T(8,128)(2,1)S(1)}, bf16[272,128]{1,0:T(8,128)(2,1)S(1)}, u32[]{:S(2)}, u32[]{:S(2)}) collective-permute-start(bf16[272,128]{1,0:T(8,128)(2,1)S(1)} %get-tuple-element.34), channel_id=1, source_target_pairs={{0,22},{2,20},{4,18},{6,16},{8,30},{10,28},{12,26},{14,24},{16,6},... | collective-permute-start | bytes 208904 | tf_op jit(solution)/shard_map/ppermute | solution.py:323
  35.5 0.0 collective-permute-done.7.refs_3_
  35.5 3.0 %core.6 = (f32[512,256]{1,0:T(8,128)S(1)}, f32[512,256]{1,0:T(8,128)S(1)}) custom-call(s32[1]{0:T(128)} %bitcast.flip_ref, s32[256,128]{1,0:T(8,128)S(1)} %copy-done, bf16[32,128]{1,0:T(8,128)(2,1)S(1)} %bitcast.7, bf16[272,128]{1,0:T(8,128)(2,1)S(1)} %collective-permute-done.4.refs_0_, ...), custom_call_target="tpu_custom_call", output_to_operand_aliasing={{0}: (7, {}), {1}: (8, {})} | custom-call | flops 2147483648 | bytes 1327104 | tf_op jit(solution)/shard_map/core/pallas_call | solution.py:243
  38.5 3.7 %collective-permute-done.2.refs_0_ = bf16[272,128]{1,0:T(8,128)(2,1)S(1)} collective-permute-done((bf16[272,128]{1,0:T(8,128)(2,1)S(1)}, bf16[272,128]{1,0:T(8,128)(2,1)S(1)}, u32[]{:S(2)}, u32[]{:S(2)}) %collective-permute-start.2) | collective-permute-done | bytes 69664 | tf_op jit(solution)/shard_map/ppermute | solution.py:323
  42.2 2.4 %collective-permute-done.3.refs_1_ = bf16[272,128]{1,0:T(8,128)(2,1)S(1)} collective-permute-done((bf16[272,128]{1,0:T(8,128)(2,1)S(1)}, bf16[272,128]{1,0:T(8,128)(2,1)S(1)}, u32[]{:S(2)}, u32[]{:S(2)}) %collective-permute-start.3) | collective-permute-done | bytes 69664 | tf_op jit(solution)/shard_map/ppermute | solution.py:323
  44.6 1.6 %core.7 = (f32[512,256]{1,0:T(8,128)S(1)}, f32[512,256]{1,0:T(8,128)S(1)}) custom-call(s32[1]{0:T(128)} %bitcast.flip_ref, s32[256,128]{1,0:T(8,128)S(1)} %copy-done, bf16[32,128]{1,0:T(8,128)(2,1)S(1)} %bitcast.8, bf16[272,128]{1,0:T(8,128)(2,1)S(1)} %collective-permute-done.2.refs_0_, ...), custom_call_target="tpu_custom_call", output_to_operand_aliasing={{0}: (5, {}), {1}: (6, {})} | custom-call | flops 1073741824 | bytes 1187840 | tf_op jit(solution)/shard_map/core/pallas_call | solution.py:243
  46.3 0.0 collective-permute-done.refs_0_
  46.3 0.0 collective-permute-done.1.refs_1_
  46.3 1.1 %core.9 = bf16[512,256]{1,0:T(8,128)(2,1)S(1)} custom-call(s32[1]{0:T(128)} %bitcast.flip_ref, s32[256,128]{1,0:T(8,128)S(1)} %copy-done, bf16[32,128]{1,0:T(8,128)(2,1)S(1)} %bitcast.9, bf16[272,128]{1,0:T(8,128)(2,1)S(1)} %collective-permute-done.refs_0_, bf16[272,128]{1,0:T(8,128)(2,1)S(1)} %collective-permute-done.1.refs_1_, ...), custom_call_target="tpu_custom_call" | custom-call | flops 536870912 | bytes 663552 | tf_op jit(solution)/shard_map/core/pallas_call | solution.py:243
  47.3 1.6 %collective-permute-start.15 = (bf16[512,256]{1,0:T(8,128)(2,1)S(1)}, bf16[512,256]{1,0:T(8,128)(2,1)S(1)}, u32[]{:S(2)}, u32[]{:S(2)}) collective-permute-start(bf16[512,256]{1,0:T(8,128)(2,1)S(1)} %core.9), channel_id=1, source_target_pairs={{0,1},{1,0},{2,3},{3,2},{4,5},{5,4},{6,7},{7,6},{8,9},{9,8},{10,11... | collective-permute-start | bytes 786440 | tf_op jit(solution)/shard_map/ppermute | solution.py:345
  48.9 1.2 %core.8.keep_ref = f32[512,256]{1,0:T(8,128)S(1)} custom-call(s32[1]{0:T(128)} %bitcast.flip_ref, s32[256,128]{1,0:T(8,128)S(1)} %copy-done, bf16[32,128]{1,0:T(8,128)(2,1)S(1)} %bitcast.10, bf16[272,128]{1,0:T(8,128)(2,1)S(1)} %collective-permute-done.refs_0_, bf16[272,128]{1,0:T(8,128)(2,1)S(1)} %collective-permute-done.1.refs_1_, ...), custom_call_target="tpu_custom_call", output_to_operand_aliasing={{}: (5, {})} | custom-call | flops 536870912 | bytes 663552 | tf_op jit(solution)/shard_map/core/pallas_call | solution.py:243
  50.1 5.6 %collective-permute-done.15.got_ref = bf16[512,256]{1,0:T(8,128)(2,1)S(1)} collective-permute-done((bf16[512,256]{1,0:T(8,128)(2,1)S(1)}, bf16[512,256]{1,0:T(8,128)(2,1)S(1)}, u32[]{:S(2)}, u32[]{:S(2)}) %collective-permute-start.15) | collective-permute-done | bytes 262176 | tf_op jit(solution)/shard_map/ppermute | solution.py:345
  55.7 1.2 %finish.1 = bf16[128,1024]{1,0:T(8,128)(2,1)} custom-call(f32[512,256]{1,0:T(8,128)S(1)} %core.8.keep_ref, bf16[512,256]{1,0:T(8,128)(2,1)S(1)} %collective-permute-done.15.got_ref), custom_call_target="tpu_custom_call" | custom-call | tf_op jit(solution)/shard_map/finish/pallas_call | solution.py:347
Async XLA Ops:
  4.3 21.7 %copy-start = (s32[256,128]{1,0:T(8,128)S(1)}, s32[256,128]{1,0:T(8,128)}, u32[]{:S(2)}) copy-start(s32[256,128]{1,0:T(8,128)} %sampled_ref.9) | copy-start | bytes 393220
  7.0 5.0 %collective-permute-start.8 = (bf16[272,128]{1,0:T(8,128)(2,1)S(1)}, bf16[272,128]{1,0:T(8,128)(2,1)S(1)}, u32[]{:S(2)}, u32[]{:S(2)}) collective-permute-start(bf16[272,128]{1,0:T(8,128)(2,1)S(1)} %get-tuple-element.44), channel_id=1, source_target_pairs={{0,2},{2,0},{4,6},{6,4},{8,10},{10,8},{12,14},{14,12},{16,18},{18,... | collective-permute-start | bytes 208904 | tf_op jit(solution)/shard_map/ppermute | solution.py:323
  7.5 7.1 %collective-permute-start.9 = (bf16[272,128]{1,0:T(8,128)(2,1)S(1)}, bf16[272,128]{1,0:T(8,128)(2,1)S(1)}, u32[]{:S(2)}, u32[]{:S(2)}) collective-permute-start(bf16[272,128]{1,0:T(8,128)(2,1)S(1)} %get-tuple-element.45), channel_id=1, source_target_pairs={{0,4},{2,6},{4,0},{6,2},{8,12},{10,14},{12,8},{14,10},{16,20},{18,... | collective-permute-start | bytes 208904 | tf_op jit(solution)/shard_map/ppermute | solution.py:323
  10.0 4.8 %collective-permute-start.10 = (bf16[272,128]{1,0:T(8,128)(2,1)S(1)}, bf16[272,128]{1,0:T(8,128)(2,1)S(1)}, u32[]{:S(2)}, u32[]{:S(2)}) collective-permute-start(bf16[272,128]{1,0:T(8,128)(2,1)S(1)} %get-tuple-element.46), channel_id=1, source_target_pairs={{0,6},{2,4},{4,2},{6,0},{8,14},{10,12},{12,10},{14,8},{16,22},{18,... | collective-permute-start | bytes 208904 | tf_op jit(solution)/shard_map/ppermute | solution.py:323
  10.1 8.2 %collective-permute-start.11 = (bf16[272,128]{1,0:T(8,128)(2,1)S(1)}, bf16[272,128]{1,0:T(8,128)(2,1)S(1)}, u32[]{:S(2)}, u32[]{:S(2)}) collective-permute-start(bf16[272,128]{1,0:T(8,128)(2,1)S(1)} %get-tuple-element.47), channel_id=1, source_target_pairs={{0,8},{2,10},{4,12},{6,14},{8,0},{10,2},{12,4},{14,6},{16,24},{18,... | collective-permute-start | bytes 208904 | tf_op jit(solution)/shard_map/ppermute | solution.py:323
  11.9 6.4 %collective-permute-start.12 = (bf16[272,128]{1,0:T(8,128)(2,1)S(1)}, bf16[272,128]{1,0:T(8,128)(2,1)S(1)}, u32[]{:S(2)}, u32[]{:S(2)}) collective-permute-start(bf16[272,128]{1,0:T(8,128)(2,1)S(1)} %get-tuple-element.48), channel_id=1, source_target_pairs={{0,10},{2,8},{4,14},{6,12},{8,2},{10,0},{12,6},{14,4},{16,26},{18,... | collective-permute-start | bytes 208904 | tf_op jit(solution)/shard_map/ppermute | solution.py:323
  11.9 10.2 %collective-permute-start.13 = (bf16[272,128]{1,0:T(8,128)(2,1)S(1)}, bf16[272,128]{1,0:T(8,128)(2,1)S(1)}, u32[]{:S(2)}, u32[]{:S(2)}) collective-permute-start(bf16[272,128]{1,0:T(8,128)(2,1)S(1)} %get-tuple-element.49), channel_id=1, source_target_pairs={{0,12},{2,14},{4,8},{6,10},{8,4},{10,6},{12,0},{14,2},{16,28},{18,... | collective-permute-start | bytes 208904 | tf_op jit(solution)/shard_map/ppermute | solution.py:323
  14.6 8.3 %collective-permute-start.14 = (bf16[272,128]{1,0:T(8,128)(2,1)S(1)}, bf16[272,128]{1,0:T(8,128)(2,1)S(1)}, u32[]{:S(2)}, u32[]{:S(2)}) collective-permute-start(bf16[272,128]{1,0:T(8,128)(2,1)S(1)} %get-tuple-element.50), channel_id=1, source_target_pairs={{0,14},{2,12},{4,10},{6,8},{8,6},{10,4},{12,2},{14,0},{16,30},{18,... | collective-permute-start | bytes 208904 | tf_op jit(solution)/shard_map/ppermute | solution.py:323
  14.8 11.1 %copy-start.1 = (bf16[128,32]{0,1:T(8,128)(2,1)S(1)}, bf16[128,32]{0,1:T(8,128)(2,1)}, u32[]{:S(2)}) copy-start(bf16[128,32]{0,1:T(8,128)(2,1)} %param.11) | copy-start | bytes 24580
  14.9 31.4 %collective-permute-start = (bf16[272,128]{1,0:T(8,128)(2,1)S(1)}, bf16[272,128]{1,0:T(8,128)(2,1)S(1)}, u32[]{:S(2)}, u32[]{:S(2)}) collective-permute-start(bf16[272,128]{1,0:T(8,128)(2,1)S(1)} %get-tuple-element.31), channel_id=1, source_target_pairs={{0,26},{2,24},{4,30},{6,28},{8,18},{10,16},{12,22},{14,20},{16,10}... | collective-permute-start | bytes 208904 | tf_op jit(solution)/shard_map/ppermute | solution.py:323
  18.3 13.0 %collective-permute-start.4 = (bf16[272,128]{1,0:T(8,128)(2,1)S(1)}, bf16[272,128]{1,0:T(8,128)(2,1)S(1)}, u32[]{:S(2)}, u32[]{:S(2)}) collective-permute-start(bf16[272,128]{1,0:T(8,128)(2,1)S(1)} %get-tuple-element.35), channel_id=1, source_target_pairs={{0,16},{2,18},{4,20},{6,22},{8,24},{10,26},{12,28},{14,30},{16,0},... | collective-permute-start | bytes 208904 | tf_op jit(solution)/shard_map/ppermute | solution.py:323
  18.3 14.5 %collective-permute-start.5 = (bf16[272,128]{1,0:T(8,128)(2,1)S(1)}, bf16[272,128]{1,0:T(8,128)(2,1)S(1)}, u32[]{:S(2)}, u32[]{:S(2)}) collective-permute-start(bf16[272,128]{1,0:T(8,128)(2,1)S(1)} %get-tuple-element.36), channel_id=1, source_target_pairs={{0,20},{2,22},{4,16},{6,18},{8,28},{10,30},{12,24},{14,26},{16,4},... | collective-permute-start | bytes 208904 | tf_op jit(solution)/shard_map/ppermute | solution.py:323
  22.2 10.7 %collective-permute-start.6 = (bf16[272,128]{1,0:T(8,128)(2,1)S(1)}, bf16[272,128]{1,0:T(8,128)(2,1)S(1)}, u32[]{:S(2)}, u32[]{:S(2)}) collective-permute-start(bf16[272,128]{1,0:T(8,128)(2,1)S(1)} %get-tuple-element.37), channel_id=1, source_target_pairs={{0,24},{2,26},{4,28},{6,30},{8,16},{10,18},{12,20},{14,22},{16,8},... | collective-permute-start | bytes 208904 | tf_op jit(solution)/shard_map/ppermute | solution.py:323
  22.9 12.6 %collective-permute-start.7 = (bf16[272,128]{1,0:T(8,128)(2,1)S(1)}, bf16[272,128]{1,0:T(8,128)(2,1)S(1)}, u32[]{:S(2)}, u32[]{:S(2)}) collective-permute-start(bf16[272,128]{1,0:T(8,128)(2,1)S(1)} %get-tuple-element.38), channel_id=1, source_target_pairs={{0,28},{2,30},{4,24},{6,26},{8,20},{10,22},{12,16},{14,18},{16,12}... | collective-permute-start | bytes 208904 | tf_op jit(solution)/shard_map/ppermute | solution.py:323
  31.3 15.0 %collective-permute-start.1 = (bf16[272,128]{1,0:T(8,128)(2,1)S(1)}, bf16[272,128]{1,0:T(8,128)(2,1)S(1)}, u32[]{:S(2)}, u32[]{:S(2)}) collective-permute-start(bf16[272,128]{1,0:T(8,128)(2,1)S(1)} %get-tuple-element.32), channel_id=1, source_target_pairs={{0,30},{2,28},{4,26},{6,24},{8,22},{10,20},{12,18},{14,16},{16,14}... | collective-permute-start | bytes 208904 | tf_op jit(solution)/shard_map/ppermute | solution.py:323
  32.9 9.4 %collective-permute-start.2 = (bf16[272,128]{1,0:T(8,128)(2,1)S(1)}, bf16[272,128]{1,0:T(8,128)(2,1)S(1)}, u32[]{:S(2)}, u32[]{:S(2)}) collective-permute-start(bf16[272,128]{1,0:T(8,128)(2,1)S(1)} %get-tuple-element.33), channel_id=1, source_target_pairs={{0,18},{2,16},{4,22},{6,20},{8,26},{10,24},{12,30},{14,28},{16,2},... | collective-permute-start | bytes 208904 | tf_op jit(solution)/shard_map/ppermute | solution.py:323
  32.9 11.8 %collective-permute-start.3 = (bf16[272,128]{1,0:T(8,128)(2,1)S(1)}, bf16[272,128]{1,0:T(8,128)(2,1)S(1)}, u32[]{:S(2)}, u32[]{:S(2)}) collective-permute-start(bf16[272,128]{1,0:T(8,128)(2,1)S(1)} %get-tuple-element.34), channel_id=1, source_target_pairs={{0,22},{2,20},{4,18},{6,16},{8,30},{10,28},{12,26},{14,24},{16,6},... | collective-permute-start | bytes 208904 | tf_op jit(solution)/shard_map/ppermute | solution.py:323
  47.3 8.4 %collective-permute-start.15 = (bf16[512,256]{1,0:T(8,128)(2,1)S(1)}, bf16[512,256]{1,0:T(8,128)(2,1)S(1)}, u32[]{:S(2)}, u32[]{:S(2)}) collective-permute-start(bf16[512,256]{1,0:T(8,128)(2,1)S(1)} %core.9), channel_id=1, source_target_pairs={{0,1},{1,0},{2,3},{3,2},{4,5},{5,4},{6,7},{7,6},{8,9},{9,8},{10,11... | collective-permute-start | bytes 786440 | tf_op jit(solution)/shard_map/ppermute | solution.py:345

commit v4 on v3

--- a/solution.py
+++ b/solution.py
@@ -26,6 +26,12 @@
     return lax.dot_general(
         lhs, rhs, (((1,), (0,)), ((), ())), preferred_element_type=F32
     )
+
+
+def chip_masks(owners):
+    chips = owners // 4
+    far = range(chips, 2 * chips)
+    return list(far[0::2]), list(far[1::2]), list(range(1, chips))
 
 
 def place_rows(owners, me, owner_ref, place_ref):
@@ -50,11 +56,11 @@
 
 
 def put_rows(
-    first, capacity, echo_local, me, reduced_ref, owner_ref, slot_ref, place_ref,
-    out_refs, spread_ref, hot_ref, ids_ref,
+    wanted, capacity, echo_local, me, reduced_ref, owner_ref, slot_ref, place_ref,
+    slots, spread_ref, hot_ref, ids_ref,
 ):
     rank, rows = reduced_ref.shape
-    count = len(out_refs)
+    count = len(slots)
     groups = capacity // LANES
     lane_range = lax.broadcasted_iota(I32, (LANES, STEP), 0).astype(F32).astype(BF16)
     group_range = lax.broadcasted_iota(I32, (8, STEP), 0)
@@ -86,35 +92,39 @@
         owner_c = level(relative, 16)
         for o in range(count):
             spread_ref[o * rank : (o + 1) * rank, at] = jnp.where(
-                owner_b == BF16(first + o), reduced, BF16(0)
+                owner_b == BF16(wanted[o]), reduced, BF16(0)
             )
         spread_ids = jnp.concatenate(
             [
-                jnp.where(owner_c == BF16(first + o), ids, BF16(0))
+                jnp.where(owner_c == BF16(wanted[o]), ids, BF16(0))
                 for o in range(count)
             ],
             axis=0,
         )
         part = nt_dot(spread_ids, lane_hot)
         ids_ref[...] = part if j == 0 else ids_ref[...] + part
-    for o in range(count):
-        out_refs[o][groups * rank :, :] = ids_ref[o * 16 : (o + 1) * 16, :].astype(BF16)
+    for o, (out_ref, base) in enumerate(slots):
+        base += groups * rank
+        out_ref[base : base + 16, :] = ids_ref[o * 16 : (o + 1) * 16, :].astype(BF16)
     wide = 2 * LANES
     for g in range(0, groups, 2):
         made = nt_dot(spread_ref[...], hot_ref[g * LANES : g * LANES + wide, :]).astype(BF16)
-        for o in range(count):
+        for o, (out_ref, base) in enumerate(slots):
             for i in range(2):
-                out_refs[o][(g + i) * rank : (g + i + 1) * rank, :] = made[
+                at = base + (g + i) * rank
+                out_ref[at : at + rank, :] = made[
                     o * rank : (o + 1) * rank, i * LANES : (i + 1) * LANES
                 ]
 
 
-def far_kernel(
+def early_kernel(
     owners, capacity, echo_local, me_ref, acquired_hbm, owner_hbm, slot_hbm, left_hbm,
     reduced_ref, place_ref, owner_ref, slot_ref, *refs,
 ):
-    outs = refs[: owners // 2]
-    acquired_ref, left_ref, spread_ref, hot_ref, ids_ref, sems = refs[owners // 2 :]
+    chips = owners // 4
+    pairs, refs = refs[: chips // 2], refs[chips // 2 :]
+    apart_ref, acquired_ref, left_ref, spread_ref, hot_ref, ids_ref, sems = refs
+    depth = pairs[0].shape[0] // 2
     copies = [
         pltpu.make_async_copy(a, b, sems.at[i])
         for i, (a, b) in enumerate(
@@ -134,28 +144,53 @@
     for copy in copies[1:]:
         copy.wait()
     reduced_ref[...] = nt_dot(left_ref[...], acquired_ref[...]).astype(BF16)
+    early, late, close = chip_masks(owners)
+    wanted, slots = [], []
+    for m, pair in zip(early, pairs):
+        wanted += [2 * m, 2 * m + 1]
+        slots += [(pair, 0), (pair, depth)]
+    for i, m in enumerate([0, *late, *close]):
+        wanted.append(2 * m + 1)
+        slots.append((apart_ref, i * depth))
     put_rows(
-        owners // 2, capacity, echo_local, me, reduced_ref, owner_ref, slot_ref, place_ref,
-        outs, spread_ref, hot_ref, ids_ref,
-    )
-
-
-def near_kernel(
-    owners, capacity, echo_local, me_ref, owner_ref, slot_ref, reduced_ref, place_ref, *refs
+        wanted, capacity, echo_local, me, reduced_ref, owner_ref, slot_ref, place_ref,
+        slots, spread_ref, hot_ref, ids_ref,
+    )
+
+
+def rest_kernel(
+    owners, capacity, echo_local, me_ref, owner_ref, slot_ref, reduced_ref, place_ref,
+    other_ref, own_ref, *refs,
 ):
+    _, late, close = chip_masks(owners)
+    masks = [*late, *close]
+    joined, scratch = refs[: len(masks)], refs[len(masks) :]
+    depth = own_ref.shape[0]
+    for i, ref in enumerate(joined):
+        ref[depth:, :] = other_ref[(i + 1) * depth : (i + 2) * depth, :]
     put_rows(
-        0, capacity, echo_local, me_ref[0], reduced_ref, owner_ref, slot_ref, place_ref,
-        refs[: owners // 2], *refs[owners // 2 :],
-    )
-
-
-def core_kernel(count, halves, more, flip_ref, sampled_ref, right_ref, *refs):
-    blocks, refs = refs[:count], refs[count:]
+        [0, *[2 * m for m in masks]], capacity, echo_local, me_ref[0],
+        reduced_ref, owner_ref, slot_ref, place_ref,
+        [(own_ref, 0), *[(ref, 0) for ref in joined]], *scratch,
+    )
+
+
+def core_kernel(
+    plan, depth, halves, more, flip_ref, sampled_ref, right_ref, *refs
+):
+    arrays, refs = refs[: len(plan)], refs[len(plan) :]
+    blocks = [(r, i * depth) for r, p in zip(arrays, plan) for i in p[0]]
+    onward = [(r, i * depth) for r, p in zip(arrays, plan) for i in p[1]]
     before = refs[: len(halves)] if more else None
     refs = refs[len(halves) :] if more else refs
-    outs, (a_ref, b_ref) = refs[: len(halves)], refs[len(halves) :]
+    outs, refs = refs[: len(halves)], refs[len(halves) :]
+    if onward:
+        for out_ref, (ref, base) in zip(refs, onward):
+            out_ref[...] = ref[base : base + depth, :]
+        refs = refs[len(onward) :]
+    a_ref, b_ref = refs
     rank = right_ref.shape[0]
-    groups = (blocks[0].shape[0] - 16) // rank
+    groups = (depth - 16) // rank
     size = groups * LANES
     half = FINE // 2
     flip = flip_ref[0] * half
@@ -166,10 +201,10 @@
     table = jnp.concatenate([right_ref[...], bits.astype(F32).astype(BF16)], axis=0)
     echo_range = lax.broadcasted_iota(I32, (echo_local, LANES), 0).astype(F32).astype(BF16)
     bit_range = lax.broadcasted_iota(I32, (32, LANES), 0)
-    for s, block in enumerate(blocks):
-        ids = block[groups * rank :, :].astype(F32)
+    for s, (ref, base) in enumerate(blocks):
+        ids = ref[base + groups * rank : base + depth, :].astype(F32)
         for g in range(groups):
-            feature = block[g * rank : (g + 1) * rank, :]
+            feature = ref[base + g * rank : base + (g + 1) * rank, :]
             voxel = ids[g : g + 1].astype(I32)
             echo = jnp.broadcast_to(ids[8 + g : 9 + g], (echo_local, LANES)).astype(BF16)
             echo_hot = jnp.where(echo == echo_range, BF16(1), BF16(0))
@@ -233,18 +268,24 @@
 PARAMS = pltpu.CompilerParams(vmem_limit_bytes=40 * 2**20)
 
 
-def core_call(blocks, flip, sampled, right, halves=(0, 1), before=(), kinds=None):
+def core_call(
+    arrays, plan, depth, flip, sampled, right, halves=(0, 1), before=(), kinds=None
+):
     rank = right.shape[0]
-    groups = (blocks[0].shape[0] - 16) // rank
-    rows = len(blocks) * groups * LANES
+    groups = (depth - 16) // rank
+    count = sum(len(p[0]) for p in plan)
+    onward = sum(len(p[1]) for p in plan)
+    rows = count * groups * LANES
     wide, narrow = FINE * rank, FINE * rank // 2
-    first = 3 + len(blocks)
+    first = 3 + len(arrays)
     kinds = kinds or [F32] * len(halves)
+    shapes = [jax.ShapeDtypeStruct((wide, narrow), kind) for kind in kinds]
+    shapes += [jax.ShapeDtypeStruct((depth, LANES), BF16)] * onward
     return pl.pallas_call(
-        functools.partial(core_kernel, len(blocks), halves, bool(before)),
-        out_shape=[jax.ShapeDtypeStruct((wide, narrow), kind) for kind in kinds],
-        in_specs=[SMEM] + [VMEM] * (2 + len(blocks) + len(before)),
-        out_specs=[VMEM] * len(halves),
+        functools.partial(core_kernel, plan, depth, halves, bool(before)),
+        out_shape=shapes,
+        in_specs=[SMEM] + [VMEM] * (2 + len(arrays) + len(before)),
+        out_specs=[VMEM] * len(shapes),
         scratch_shapes=[
             pltpu.VMEM((wide, rows), BF16),
             pltpu.VMEM((narrow * len(halves), rows), BF16),
@@ -253,13 +294,9 @@
             first + i: i for i in range(len(before)) if kinds[i] == F32
         },
         compiler_params=PARAMS,
-        cost_estimate=pl.CostEstimate(
-            flops=2 * rows * wide * narrow * len(halves),
-            bytes_accessed=rows * 68 + 4 * wide * narrow * len(halves),
-            transcendentals=0,
-        ),
+        cost_estimate=pl.CostEstimate(flops=1, bytes_accessed=1, transcendentals=0),
         name="core",
-    )(flip, sampled, right, *blocks, *before)
+    )(flip, sampled, right, *arrays, *before)
 
 
 def on_device(acquired, owner, slot, sampled, left_panel, right_panel):
@@ -271,79 +308,96 @@
     vox_local, echo_local = sampled.shape
     rank = left_panel.shape[1]
     depth = groups * rank + 16
-    half = owners // 2
+    early, late, close = chip_masks(owners)
     me = lax.axis_index("vox").reshape(1)
     mine = lax.axis_index("echo")
     owner, slot = owner.reshape(1, rows), slot.reshape(1, rows)
     left, right = left_panel.T, right_panel.T
-    block = jax.ShapeDtypeStruct((depth, LANES), BF16)
-    sums = [
-        pltpu.VMEM((half * rank, rows), BF16),
-        pltpu.VMEM((capacity, rows), BF16),
-        pltpu.VMEM((half * 16, LANES), F32),
-    ]
+
+    def blocks(n):
+        return jax.ShapeDtypeStruct((n * depth, LANES), BF16)
+
+    def sent(array, mask):
+        return lax.ppermute(array, "vox", [(i, i ^ mask) for i in range(owners)])
+
+    def scratch(n):
+        return [
+            pltpu.VMEM((n * rank, rows), BF16),
+            pltpu.VMEM((capacity, rows), BF16),
+            pltpu.VMEM((n * 16, LANES), F32),
+        ]
+
     cost = pl.CostEstimate(
-        flops=2 * rows * capacity * half * rank,
+        flops=rows * capacity * owners * rank,
         bytes_accessed=4 * rows * 128,
         transcendentals=0,
     )
-    reduced, place, owner, slot, *far = pl.pallas_call(
-        functools.partial(far_kernel, owners, capacity, echo_local),
-        out_shape=[
-            jax.ShapeDtypeStruct((rank, rows), BF16),
-            jax.ShapeDtypeStruct((rows // CHUNK, 1, CHUNK), I32),
-            jax.ShapeDtypeStruct(owner.shape, I32),
-            jax.ShapeDtypeStruct(slot.shape, I32),
-        ]
-        + [block] * half,
+    across = 1 + len(late) + len(close)
+    shapes = [
+        jax.ShapeDtypeStruct((rank, rows), BF16),
+        jax.ShapeDtypeStruct((rows // CHUNK, 1, CHUNK), I32),
+        jax.ShapeDtypeStruct(owner.shape, I32),
+        jax.ShapeDtypeStruct(slot.shape, I32),
+        *[blocks(2)] * len(early),
+        blocks(across),
+    ]
+    hbm = [
+        pltpu.with_memory_space_constraint(x, pltpu.HBM)
+        for x in (acquired, owner, slot, left)
+    ]
+    reduced, place, owner, slot, *pairs, apart = pl.pallas_call(
+        functools.partial(early_kernel, owners, capacity, echo_local),
+        out_shape=shapes,
         in_specs=[SMEM, HBM, HBM, HBM, HBM],
-        out_specs=[VMEM] * (4 + half),
+        out_specs=[VMEM] * len(shapes),
         scratch_shapes=[
             pltpu.VMEM(acquired.shape, BF16),
             pltpu.VMEM(left.shape, BF16),
-            *sums,
+            *scratch(2 * len(early) + across),
             pltpu.SemaphoreType.DMA((4,)),
         ],
         compiler_params=PARAMS,
         cost_estimate=cost,
-        name="far",
-    )(me, *[pltpu.with_memory_space_constraint(x, pltpu.HBM) for x in (acquired, owner, slot, left)])
-    near = pl.pallas_call(
-        functools.partial(near_kernel, owners, capacity, echo_local),
-        out_shape=[block] * half,
-        in_specs=[SMEM] + [VMEM] * 4,
-        out_specs=[VMEM] * half,
-        scratch_shapes=sums,
+        name="early",
+    )(me, *hbm)
+    other = sent(apart, 1)
+    early = [sent(pair, 2 * m) for pair, m in zip(pairs, early)]
+    shapes = [blocks(1)] + [blocks(2)] * (across - 1)
+    own, *joined = pl.pallas_call(
+        functools.partial(rest_kernel, owners, capacity, echo_local),
+        out_shape=shapes,
+        in_specs=[SMEM] + [VMEM] * 5,
+        out_specs=[VMEM] * len(shapes),
+        scratch_shapes=scratch(across),
         compiler_params=PARAMS,
         cost_estimate=cost,
-        name="near",
-    )(me, owner, slot, reduced, place)
-
-    def sent(array, mask):
-        return lax.ppermute(array, "vox", [(i, i ^ mask) for i in range(owners)])
-
-    order = [*range(half, owners, 2), *range(half + 1, owners, 2)]
-    arrived = {m: sent(far[m - half], m) for m in order}
-    arrived.update({m: sent(near[m], m) if m else near[0] for m in range(half)})
+        name="rest",
+    )(me, owner, slot, reduced, place, other)
+    late = [sent(x, 2 * m) for x, m in zip(joined, late)]
+    close = [sent(x, 2 * m) for x, m in zip(joined[len(late) :], close)]
     two = shares == 2
     flip = ((1 - mine) if two else jnp.zeros((), I32)).astype(I32).reshape(1)
-    run = functools.partial(core_call, flip=flip, sampled=sampled, right=right)
-    total = run([arrived[m] for m in range(half)])
-    late = order[-2:]
-    done = order[:-2]
-    for i in range(0, len(done), 4):
-        total = run([arrived[m] for m in done[i : i + 4]], before=total)
-    last = [arrived[m] for m in late]
+    run = functools.partial(core_call, depth=depth, flip=flip, sampled=sampled, right=right)
+    one, split, whole = ((0,), ()), ((0,), (1,)), ((0, 1), ())
+    give, keep, *onward = run([own, other, *early], [one, one, *[split] * len(early)])
+    onward = [sent(x, 1) for x in onward]
+    total = run(close, [whole] * len(close), before=(give, keep))
+    total = run(
+        [*onward, *late[:-1]],
+        [one] * len(onward) + [whole] * (len(late) - 1),
+        before=total,
+    )
+    last = functools.partial(run, late[-1:], [whole])
     share = vox_local // shares
     if not two:
-        both = jnp.concatenate(run(last, before=total), axis=1)
+        both = jnp.concatenate(last(before=total), axis=1)
         both = both.reshape(FINE * rank, shares, FINE * rank // shares)
         both = lax.psum_scatter(both, "echo", scatter_dimension=1)
         both = both.reshape(FINE, rank, FINE // shares, rank).transpose(2, 0, 1, 3)
         return both.reshape(share, rank * rank).astype(BF16)
-    (give,) = run(last, halves=(0,), before=total[:1], kinds=[BF16])
+    (give,) = last(halves=(0,), before=total[:1], kinds=[BF16])
     got = lax.ppermute(give, "echo", [(0, 1), (1, 0)])
-    (keep,) = run(last, halves=(1,), before=total[1:])
+    (keep,) = last(halves=(1,), before=total[1:])
     return pl.pallas_call(
         functools.partial(finish_kernel, rank),
         out_shape=jax.ShapeDtypeStruct((share, rank * rank), BF16),

time: 57.2 us -> 45.6 us (0.80)
  starting transfers between devices: 23.3 us -> 15.6 us
  waiting for transfers between devices: 13.2 us -> 8.43 us
  Pallas kernels: 20.3 us -> 21.3 us
    ppermute x15 -> x10, starting transfers between devices: 21.7 us -> 14 us  [sent(): return lax.ppermute(array, 'vox', [(i, i ^ mask) for i in range(owners)])]
    ppermute x15 -> x10, waiting for transfers between devices: 7.63 us -> 4.71 us  [sent(): return lax.ppermute(array, 'vox', [(i, i ^ mask) for i in range(owners)])]
    ppermute x1, waiting for transfers between devices: 5.61 us -> 3.72 us  [on_device(): got = lax.ppermute(give, 'echo', [(0, 1), (1, 0)])]
    pallas_call x7, Pallas kernels: 19.1 us -> 20.1 us  [the longest x5 12.1 us: core_call(): pl.pallas_call(functools.partial(core_kernel, plan, depth, halves, bool(b...]
  transfers between devices with their start and end apart: 16 -> 11, of which waited for: 4 -> 4; matrix products, arithmetic and copies ran while one was open for 0% -> 0% of each run, Pallas kernels for 20% -> 31%
where the time goes in v4:
time: 45.6 us; the launch traced here: 45.4 us
  Pallas kernels  21.3 us (47%)
  starting transfers between devices  15.6 us (34%)
  waiting for transfers between devices  8.43 us (18%)
    ppermute x10, starting transfers between devices, sent(): return lax.ppermute(array, 'vox', [(i, i ^ mask) for i in range(owners)])  14 us
    pallas_call x5, Pallas kernels, core_call(): pl.pallas_call(functools.partial(core_kernel, plan, depth, halves, bool(b...  12.1 us
    pallas_call x1, Pallas kernels, on_device(): pl.pallas_call(functools.partial(early_kernel, owners, capacity, echo_loc...  4.88 us
    ppermute x10, waiting for transfers between devices, sent(): return lax.ppermute(array, 'vox', [(i, i ^ mask) for i in range(owners)])  4.71 us
    ppermute x1, waiting for transfers between devices, on_device(): got = lax.ppermute(give, 'echo', [(0, 1), (1, 0)])  3.72 us
    pallas_call x1, Pallas kernels, on_device(): pl.pallas_call(functools.partial(rest_kernel, owners, capacity, echo_loca...  3.16 us
    ppermute x1, starting transfers between devices, on_device(): got = lax.ppermute(give, 'echo', [(0, 1), (1, 0)])  1.6 us
    pallas_call x1, Pallas kernels, on_device(): pl.pallas_call(functools.partial(finish_kernel, rank), out_shape=jax.Shap...  1.18 us
  transfers between devices with their start and end apart: 11, of which 4 were waited for; matrix products, arithmetic and copies ran while one was open for 0% of the time, Pallas kernels for 31%

profile of v4, /device:TPU:0, one launch (start us, length us, event | category | flops | bytes accessed | tf_op | source)
XLA Modules:
  0.0 45.4 jit_solution(6213440757716523791)
XLA Ops:
  0.0 4.9 %early.1 = (bf16[32,4096]{1,0:T(8,128)(2,1)S(1)}, s32[8,1,512]{2,1,0:T(1,128)S(1)}, s32[1,4096]{1,0:T(1,128)S(1)}, s32[1,4096]{1,0:T(1,128)S(1)}, bf16[544,128]{...) custom-call(s32[1]{0:T(128)} %bitcast.2.me_ref, bf16[4096,128]{1,0:T(8,128)(2,1)} %acquired_hbm.1, ...), custom_call_target="tpu_custom_call" | custom-call | flops 2147483648 | bytes 2097152 | tf_op jit(solution)/shard_map/early/pallas_call | solution.py:348
  4.9 0.5 %collective-permute-start = (bf16[1632,128]{1,0:T(8,128)(2,1)S(1)}, bf16[1632,128]{1,0:T(8,128)(2,1)S(1)}, u32[]{:S(2)}, u32[]{:S(2)}) collective-permute-start(bf16[1632,128]{1,0:T(8,128)(2,1)S(1)} %get-tuple-element.30), channel_id=1, source_target_pairs={{0,2},{2,0},{4,6},{6,4},{8,10},{10,8},{12,14},{14,12},{16,18},{18,... | collective-permute-start | bytes 1253384 | tf_op jit(solution)/shard_map/ppermute | solution.py:321
  5.4 3.7 %collective-permute-start.2 = (bf16[544,128]{1,0:T(8,128)(2,1)S(1)}, bf16[544,128]{1,0:T(8,128)(2,1)S(1)}, u32[]{:S(2)}, u32[]{:S(2)}) collective-permute-start(bf16[544,128]{1,0:T(8,128)(2,1)S(1)} %get-tuple-element.33), channel_id=1, source_target_pairs={{0,16},{2,18},{4,20},{6,22},{8,24},{10,26},{12,28},{14,30},{16,0},... | collective-permute-start | bytes 417800 | tf_op jit(solution)/shard_map/ppermute | solution.py:321
  9.1 1.3 %collective-permute-start.3 = (bf16[544,128]{1,0:T(8,128)(2,1)S(1)}, bf16[544,128]{1,0:T(8,128)(2,1)S(1)}, u32[]{:S(2)}, u32[]{:S(2)}) collective-permute-start(bf16[544,128]{1,0:T(8,128)(2,1)S(1)} %get-tuple-element.34), channel_id=1, source_target_pairs={{0,24},{2,26},{4,28},{6,30},{8,16},{10,18},{12,20},{14,22},{16,8},... | collective-permute-start | bytes 417800 | tf_op jit(solution)/shard_map/ppermute | solution.py:321
  10.4 0.0 collective-permute-done.other_ref.refs_1_
  10.4 0.0 copy-start
  10.4 3.2 %rest.1 = (bf16[272,128]{1,0:T(8,128)(2,1)S(1)}, bf16[544,128]{1,0:T(8,128)(2,1)S(1)}, bf16[544,128]{1,0:T(8,128)(2,1)S(1)}, bf16[544,128]{1,0:T(8,128)(2,1)S(1)...) custom-call(s32[1]{0:T(128)} %bitcast.2.me_ref, s32[1,4096]{1,0:T(1,128)S(1)} %get-tuple-element.26.owner_ref, ...), custom_call_target="tpu_custom_call" | custom-call | flops 2147483648 | bytes 2097152 | tf_op jit(solution)/shard_map/rest/pallas_call | solution.py:366
  13.6 1.6 %collective-permute-start.7 = (bf16[544,128]{1,0:T(8,128)(2,1)S(1)}, bf16[544,128]{1,0:T(8,128)(2,1)S(1)}, u32[]{:S(2)}, u32[]{:S(2)}) collective-permute-start(bf16[544,128]{1,0:T(8,128)(2,1)S(1)} %get-tuple-element.38), channel_id=1, source_target_pairs={{0,4},{2,6},{4,0},{6,2},{8,12},{10,14},{12,8},{14,10},{16,20},{18,... | collective-permute-start | bytes 417800 | tf_op jit(solution)/shard_map/ppermute | solution.py:321
  15.1 0.2 collective-permute-start.8
  15.4 0.0 copy-start.1
  15.4 1.8 %collective-permute-start.9 = (bf16[544,128]{1,0:T(8,128)(2,1)S(1)}, bf16[544,128]{1,0:T(8,128)(2,1)S(1)}, u32[]{:S(2)}, u32[]{:S(2)}) collective-permute-start(bf16[544,128]{1,0:T(8,128)(2,1)S(1)} %get-tuple-element.40), channel_id=1, source_target_pairs={{0,12},{2,14},{4,8},{6,10},{8,4},{10,6},{12,0},{14,2},{16,28},{18,... | collective-permute-start | bytes 417800 | tf_op jit(solution)/shard_map/ppermute | solution.py:321
  17.2 2.4 %collective-permute-done.2.refs_2_ = bf16[544,128]{1,0:T(8,128)(2,1)S(1)} collective-permute-done((bf16[544,128]{1,0:T(8,128)(2,1)S(1)}, bf16[544,128]{1,0:T(8,128)(2,1)S(1)}, u32[]{:S(2)}, u32[]{:S(2)}) %collective-permute-start.2) | collective-permute-done | bytes 139296 | tf_op jit(solution)/shard_map/ppermute | solution.py:321
  19.6 0.8 %collective-permute-start.6 = (bf16[544,128]{1,0:T(8,128)(2,1)S(1)}, bf16[544,128]{1,0:T(8,128)(2,1)S(1)}, u32[]{:S(2)}, u32[]{:S(2)}) collective-permute-start(bf16[544,128]{1,0:T(8,128)(2,1)S(1)} %get-tuple-element.37), channel_id=1, source_target_pairs={{0,20},{2,22},{4,16},{6,18},{8,28},{10,30},{12,24},{14,26},{16,4},... | collective-permute-start | bytes 417800 | tf_op jit(solution)/shard_map/ppermute | solution.py:321
  20.3 0.0 collective-permute-done.3.refs_3_
  20.3 3.6 %collective-permute-start.1 = (bf16[544,128]{1,0:T(8,128)(2,1)S(1)}, bf16[544,128]{1,0:T(8,128)(2,1)S(1)}, u32[]{:S(2)}, u32[]{:S(2)}) collective-permute-start(bf16[544,128]{1,0:T(8,128)(2,1)S(1)} %get-tuple-element.31), channel_id=1, source_target_pairs={{0,28},{2,30},{4,24},{6,26},{8,20},{10,22},{12,16},{14,18},{16,12}... | collective-permute-start | bytes 417800 | tf_op jit(solution)/shard_map/ppermute | solution.py:321
  23.9 0.0 copy-done
  23.9 0.0 copy-done.1
  23.9 2.8 %core.5 = (f32[512,256]{1,0:T(8,128)S(1)}, f32[512,256]{1,0:T(8,128)S(1)}, bf16[272,128]{1,0:T(8,128)(2,1)S(1)}, bf16[272,128]{1,0:T(8,128)(2,1)S(1)}) custom-call(s32[1]{0:T(128)} %bitcast.flip_ref, s32[256,128]{1,0:T(8,128)S(1)} %copy-done, bf16[32,128]{1,0:T(8,128)(2,1)S(1)} %bitcast.6, bf16[272,128]{1,0:T(8,128)(2,1)S(1)} %get-tuple-element.32.refs_0_, ...), custom_call_target="tpu_custom_call" | custom-call | flops 1 | bytes 1 | tf_op jit(solution)/shard_map/core/pallas_call | solution.py:284
  26.7 0.0 collective-permute-done.7.refs_0_
  26.7 0.1 collective-permute-start.4
  26.8 0.0 collective-permute-done.8.refs_1_
  26.8 0.5 %collective-permute-start.5 = (bf16[272,128]{1,0:T(8,128)(2,1)S(1)}, bf16[272,128]{1,0:T(8,128)(2,1)S(1)}, u32[]{:S(2)}, u32[]{:S(2)}) collective-permute-start(bf16[272,128]{1,0:T(8,128)(2,1)S(1)} %get-tuple-element.36), channel_id=1, source_target_pairs={{0,2},{2,0},{4,6},{6,4},{8,10},{10,8},{12,14},{14,12},{16,18},{18,... | collective-permute-start | bytes 208904 | tf_op jit(solution)/shard_map/ppermute | solution.py:321
  27.3 0.5 %collective-permute-done.9.refs_2_ = bf16[544,128]{1,0:T(8,128)(2,1)S(1)} collective-permute-done((bf16[544,128]{1,0:T(8,128)(2,1)S(1)}, bf16[544,128]{1,0:T(8,128)(2,1)S(1)}, u32[]{:S(2)}, u32[]{:S(2)}) %collective-permute-start.9) | collective-permute-done | bytes 139296 | tf_op jit(solution)/shard_map/ppermute | solution.py:321
  27.8 4.3 %core.6 = (f32[512,256]{1,0:T(8,128)S(1)}, f32[512,256]{1,0:T(8,128)S(1)}) custom-call(s32[1]{0:T(128)} %bitcast.flip_ref, s32[256,128]{1,0:T(8,128)S(1)} %copy-done, bf16[32,128]{1,0:T(8,128)(2,1)S(1)} %bitcast.7, bf16[544,128]{1,0:T(8,128)(2,1)S(1)} %collective-permute-done.7.refs_0_, ...), custom_call_target="tpu_custom_call", output_to_operand_aliasing={{0}: (6, {}), {1}: (7, {})} | custom-call | flops 1 | bytes 1 | tf_op jit(solution)/shard_map/core/pallas_call | solution.py:284
  32.1 0.0 collective-permute-done.4.refs_0_
  32.1 0.0 collective-permute-done.5.refs_1_
  32.1 1.8 %collective-permute-done.6.refs_2_ = bf16[544,128]{1,0:T(8,128)(2,1)S(1)} collective-permute-done((bf16[544,128]{1,0:T(8,128)(2,1)S(1)}, bf16[544,128]{1,0:T(8,128)(2,1)S(1)}, u32[]{:S(2)}, u32[]{:S(2)}) %collective-permute-start.6) | collective-permute-done | bytes 139296 | tf_op jit(solution)/shard_map/ppermute | solution.py:321
  33.9 2.8 %core.7 = (f32[512,256]{1,0:T(8,128)S(1)}, f32[512,256]{1,0:T(8,128)S(1)}) custom-call(s32[1]{0:T(128)} %bitcast.flip_ref, s32[256,128]{1,0:T(8,128)S(1)} %copy-done, bf16[32,128]{1,0:T(8,128)(2,1)S(1)} %bitcast.8, bf16[272,128]{1,0:T(8,128)(2,1)S(1)} %collective-permute-done.4.refs_0_, ...), custom_call_target="tpu_custom_call", output_to_operand_aliasing={{0}: (6, {}), {1}: (7, {})} | custom-call | flops 1 | bytes 1 | tf_op jit(solution)/shard_map/core/pallas_call | solution.py:284
  36.7 0.0 collective-permute-done.1.refs_0_
  36.7 1.0 %core.9 = bf16[512,256]{1,0:T(8,128)(2,1)S(1)} custom-call(s32[1]{0:T(128)} %bitcast.flip_ref, s32[256,128]{1,0:T(8,128)S(1)} %copy-done, bf16[32,128]{1,0:T(8,128)(2,1)S(1)} %bitcast.9, bf16[544,128]{1,0:T(8,128)(2,1)S(1)} %collective-permute-done.1.refs_0_, f32[512,256]{1,0:T(8,128)S(1)} %get-tuple-element.46.refs_1_), custom_call_target="tpu_custom_call" | custom-call | flops 1 | bytes 1 | tf_op jit(solution)/shard_map/core/pallas_call | solution.py:284
  37.7 1.6 %collective-permute-start.10 = (bf16[512,256]{1,0:T(8,128)(2,1)S(1)}, bf16[512,256]{1,0:T(8,128)(2,1)S(1)}, u32[]{:S(2)}, u32[]{:S(2)}) collective-permute-start(bf16[512,256]{1,0:T(8,128)(2,1)S(1)} %core.9), channel_id=1, source_target_pairs={{0,1},{1,0},{2,3},{3,2},{4,5},{5,4},{6,7},{7,6},{8,9},{9,8},{10,11... | collective-permute-start | bytes 786440 | tf_op jit(solution)/shard_map/ppermute | solution.py:399
  39.3 1.2 %core.8.keep_ref = f32[512,256]{1,0:T(8,128)S(1)} custom-call(s32[1]{0:T(128)} %bitcast.flip_ref, s32[256,128]{1,0:T(8,128)S(1)} %copy-done, bf16[32,128]{1,0:T(8,128)(2,1)S(1)} %bitcast.10, bf16[544,128]{1,0:T(8,128)(2,1)S(1)} %collective-permute-done.1.refs_0_, f32[512,256]{1,0:T(8,128)S(1)} %get-tuple-element.45.refs_1_), custom_call_target="tpu_custom_call", output_to_operand_aliasing={{}: (4, {})} | custom-call | flops 1 | bytes 1 | tf_op jit(solution)/shard_map/core/pallas_call | solution.py:284
  40.5 3.7 %collective-permute-done.10.got_ref = bf16[512,256]{1,0:T(8,128)(2,1)S(1)} collective-permute-done((bf16[512,256]{1,0:T(8,128)(2,1)S(1)}, bf16[512,256]{1,0:T(8,128)(2,1)S(1)}, u32[]{:S(2)}, u32[]{:S(2)}) %collective-permute-start.10) | collective-permute-done | bytes 262176 | tf_op jit(solution)/shard_map/ppermute | solution.py:399
  44.2 1.2 %finish.1 = bf16[128,1024]{1,0:T(8,128)(2,1)} custom-call(f32[512,256]{1,0:T(8,128)S(1)} %core.8.keep_ref, bf16[512,256]{1,0:T(8,128)(2,1)S(1)} %collective-permute-done.10.got_ref), custom_call_target="tpu_custom_call" | custom-call | tf_op jit(solution)/shard_map/finish/pallas_call | solution.py:401
Async XLA Ops:
  4.9 5.5 %collective-permute-start = (bf16[1632,128]{1,0:T(8,128)(2,1)S(1)}, bf16[1632,128]{1,0:T(8,128)(2,1)S(1)}, u32[]{:S(2)}, u32[]{:S(2)}) collective-permute-start(bf16[1632,128]{1,0:T(8,128)(2,1)S(1)} %get-tuple-element.30), channel_id=1, source_target_pairs={{0,2},{2,0},{4,6},{6,4},{8,10},{10,8},{12,14},{14,12},{16,18},{18,... | collective-permute-start | bytes 1253384 | tf_op jit(solution)/shard_map/ppermute | solution.py:321
  5.4 14.2 %collective-permute-start.2 = (bf16[544,128]{1,0:T(8,128)(2,1)S(1)}, bf16[544,128]{1,0:T(8,128)(2,1)S(1)}, u32[]{:S(2)}, u32[]{:S(2)}) collective-permute-start(bf16[544,128]{1,0:T(8,128)(2,1)S(1)} %get-tuple-element.33), channel_id=1, source_target_pairs={{0,16},{2,18},{4,20},{6,22},{8,24},{10,26},{12,28},{14,30},{16,0},... | collective-permute-start | bytes 417800 | tf_op jit(solution)/shard_map/ppermute | solution.py:321
  9.1 11.3 %collective-permute-start.3 = (bf16[544,128]{1,0:T(8,128)(2,1)S(1)}, bf16[544,128]{1,0:T(8,128)(2,1)S(1)}, u32[]{:S(2)}, u32[]{:S(2)}) collective-permute-start(bf16[544,128]{1,0:T(8,128)(2,1)S(1)} %get-tuple-element.34), channel_id=1, source_target_pairs={{0,24},{2,26},{4,28},{6,30},{8,16},{10,18},{12,20},{14,22},{16,8},... | collective-permute-start | bytes 417800 | tf_op jit(solution)/shard_map/ppermute | solution.py:321
  10.4 13.5 %copy-start = (s32[256,128]{1,0:T(8,128)S(1)}, s32[256,128]{1,0:T(8,128)}, u32[]{:S(2)}) copy-start(s32[256,128]{1,0:T(8,128)} %sampled_ref.9) | copy-start | bytes 393220
  13.6 13.1 %collective-permute-start.7 = (bf16[544,128]{1,0:T(8,128)(2,1)S(1)}, bf16[544,128]{1,0:T(8,128)(2,1)S(1)}, u32[]{:S(2)}, u32[]{:S(2)}) collective-permute-start(bf16[544,128]{1,0:T(8,128)(2,1)S(1)} %get-tuple-element.38), channel_id=1, source_target_pairs={{0,4},{2,6},{4,0},{6,2},{8,12},{10,14},{12,8},{14,10},{16,20},{18,... | collective-permute-start | bytes 417800 | tf_op jit(solution)/shard_map/ppermute | solution.py:321
  15.1 11.7 %collective-permute-start.8 = (bf16[544,128]{1,0:T(8,128)(2,1)S(1)}, bf16[544,128]{1,0:T(8,128)(2,1)S(1)}, u32[]{:S(2)}, u32[]{:S(2)}) collective-permute-start(bf16[544,128]{1,0:T(8,128)(2,1)S(1)} %get-tuple-element.39), channel_id=1, source_target_pairs={{0,8},{2,10},{4,12},{6,14},{8,0},{10,2},{12,4},{14,6},{16,24},{18,... | collective-permute-start | bytes 417800 | tf_op jit(solution)/shard_map/ppermute | solution.py:321
  15.4 8.5 %copy-start.1 = (bf16[128,32]{0,1:T(8,128)(2,1)S(1)}, bf16[128,32]{0,1:T(8,128)(2,1)}, u32[]{:S(2)}) copy-start(bf16[128,32]{0,1:T(8,128)(2,1)} %param.11) | copy-start | bytes 24580
  15.4 12.4 %collective-permute-start.9 = (bf16[544,128]{1,0:T(8,128)(2,1)S(1)}, bf16[544,128]{1,0:T(8,128)(2,1)S(1)}, u32[]{:S(2)}, u32[]{:S(2)}) collective-permute-start(bf16[544,128]{1,0:T(8,128)(2,1)S(1)} %get-tuple-element.40), channel_id=1, source_target_pairs={{0,12},{2,14},{4,8},{6,10},{8,4},{10,6},{12,0},{14,2},{16,28},{18,... | collective-permute-start | bytes 417800 | tf_op jit(solution)/shard_map/ppermute | solution.py:321
  19.6 14.3 %collective-permute-start.6 = (bf16[544,128]{1,0:T(8,128)(2,1)S(1)}, bf16[544,128]{1,0:T(8,128)(2,1)S(1)}, u32[]{:S(2)}, u32[]{:S(2)}) collective-permute-start(bf16[544,128]{1,0:T(8,128)(2,1)S(1)} %get-tuple-element.37), channel_id=1, source_target_pairs={{0,20},{2,22},{4,16},{6,18},{8,28},{10,30},{12,24},{14,26},{16,4},... | collective-permute-start | bytes 417800 | tf_op jit(solution)/shard_map/ppermute | solution.py:321
  20.3 16.3 %collective-permute-start.1 = (bf16[544,128]{1,0:T(8,128)(2,1)S(1)}, bf16[544,128]{1,0:T(8,128)(2,1)S(1)}, u32[]{:S(2)}, u32[]{:S(2)}) collective-permute-start(bf16[544,128]{1,0:T(8,128)(2,1)S(1)} %get-tuple-element.31), channel_id=1, source_target_pairs={{0,28},{2,30},{4,24},{6,26},{8,20},{10,22},{12,16},{14,18},{16,12}... | collective-permute-start | bytes 417800 | tf_op jit(solution)/shard_map/ppermute | solution.py:321
  26.7 5.3 %collective-permute-start.4 = (bf16[272,128]{1,0:T(8,128)(2,1)S(1)}, bf16[272,128]{1,0:T(8,128)(2,1)S(1)}, u32[]{:S(2)}, u32[]{:S(2)}) collective-permute-start(bf16[272,128]{1,0:T(8,128)(2,1)S(1)} %get-tuple-element.35), channel_id=1, source_target_pairs={{0,2},{2,0},{4,6},{6,4},{8,10},{10,8},{12,14},{14,12},{16,18},{18,... | collective-permute-start | bytes 208904 | tf_op jit(solution)/shard_map/ppermute | solution.py:321
  26.8 5.3 %collective-permute-start.5 = (bf16[272,128]{1,0:T(8,128)(2,1)S(1)}, bf16[272,128]{1,0:T(8,128)(2,1)S(1)}, u32[]{:S(2)}, u32[]{:S(2)}) collective-permute-start(bf16[272,128]{1,0:T(8,128)(2,1)S(1)} %get-tuple-element.36), channel_id=1, source_target_pairs={{0,2},{2,0},{4,6},{6,4},{8,10},{10,8},{12,14},{14,12},{16,18},{18,... | collective-permute-start | bytes 208904 | tf_op jit(solution)/shard_map/ppermute | solution.py:321
  37.7 6.5 %collective-permute-start.10 = (bf16[512,256]{1,0:T(8,128)(2,1)S(1)}, bf16[512,256]{1,0:T(8,128)(2,1)S(1)}, u32[]{:S(2)}, u32[]{:S(2)}) collective-permute-start(bf16[512,256]{1,0:T(8,128)(2,1)S(1)} %core.9), channel_id=1, source_target_pairs={{0,1},{1,0},{2,3},{3,2},{4,5},{5,4},{6,7},{7,6},{8,9},{9,8},{10,11... | collective-permute-start | bytes 786440 | tf_op jit(solution)/shard_map/ppermute | solution.py:399

commit v5 on v4

--- a/solution.py
+++ b/solution.py
@@ -382,12 +382,8 @@
     give, keep, *onward = run([own, other, *early], [one, one, *[split] * len(early)])
     onward = [sent(x, 1) for x in onward]
     total = run(close, [whole] * len(close), before=(give, keep))
-    total = run(
-        [*onward, *late[:-1]],
-        [one] * len(onward) + [whole] * (len(late) - 1),
-        before=total,
-    )
-    last = functools.partial(run, late[-1:], [whole])
+    total = run(onward, [one] * len(onward), before=total)
+    last = functools.partial(run, late, [whole] * len(late))
     share = vox_local // shares
     if not two:
         both = jnp.concatenate(last(before=total), axis=1)

time: 45.6 us -> 45.3 us (level)
  waiting for transfers between devices: 8.43 us -> 7.55 us
    ppermute x10, waiting for transfers between devices: 4.71 us -> 3.1 us  [sent(): return lax.ppermute(array, 'vox', [(i, i ^ mask) for i in range(owners)])]
    ppermute x1, waiting for transfers between devices: 3.72 us -> 4.45 us  [on_device(): got = lax.ppermute(give, 'echo', [(0, 1), (1, 0)])]
where the time goes in v5:
time: 45.3 us; the launch traced here: 44.9 us
  Pallas kernels  21.6 us (48%)
  starting transfers between devices  15.7 us (35%)
  waiting for transfers between devices  7.55 us (17%)
    ppermute x10, starting transfers between devices, sent(): return lax.ppermute(array, 'vox', [(i, i ^ mask) for i in range(owners)])  14 us
    pallas_call x5, Pallas kernels, core_call(): pl.pallas_call(functools.partial(core_kernel, plan, depth, halves, bool(b...  12.4 us
    pallas_call x1, Pallas kernels, on_device(): pl.pallas_call(functools.partial(early_kernel, owners, capacity, echo_loc...  4.88 us
    ppermute x1, waiting for transfers between devices, on_device(): got = lax.ppermute(give, 'echo', [(0, 1), (1, 0)])  4.45 us
    pallas_call x1, Pallas kernels, on_device(): pl.pallas_call(functools.partial(rest_kernel, owners, capacity, echo_loca...  3.16 us
    ppermute x10, waiting for transfers between devices, sent(): return lax.ppermute(array, 'vox', [(i, i ^ mask) for i in range(owners)])  3.1 us
    ppermute x1, starting transfers between devices, on_device(): got = lax.ppermute(give, 'echo', [(0, 1), (1, 0)])  1.71 us
    pallas_call x1, Pallas kernels, on_device(): pl.pallas_call(functools.partial(finish_kernel, rank), out_shape=jax.Shap...  1.18 us
  transfers between devices with their start and end apart: 11, of which 4 were waited for; matrix products, arithmetic and copies ran while one was open for 0% of the time, Pallas kernels for 31%

profile of v5, /device:TPU:0, one launch (start us, length us, event | category | flops | bytes accessed | tf_op | source)
XLA Modules:
  0.0 44.9 jit_solution(15241515748072371982)
XLA Ops:
  0.0 4.9 %early.1 = (bf16[32,4096]{1,0:T(8,128)(2,1)S(1)}, s32[8,1,512]{2,1,0:T(1,128)S(1)}, s32[1,4096]{1,0:T(1,128)S(1)}, s32[1,4096]{1,0:T(1,128)S(1)}, bf16[544,128]{...) custom-call(s32[1]{0:T(128)} %bitcast.2.me_ref, bf16[4096,128]{1,0:T(8,128)(2,1)} %acquired_hbm.1, ...), custom_call_target="tpu_custom_call" | custom-call | flops 2147483648 | bytes 2097152 | tf_op jit(solution)/shard_map/early/pallas_call | solution.py:348
  4.9 0.5 %collective-permute-start = (bf16[1632,128]{1,0:T(8,128)(2,1)S(1)}, bf16[1632,128]{1,0:T(8,128)(2,1)S(1)}, u32[]{:S(2)}, u32[]{:S(2)}) collective-permute-start(bf16[1632,128]{1,0:T(8,128)(2,1)S(1)} %get-tuple-element.30), channel_id=1, source_target_pairs={{0,2},{2,0},{4,6},{6,4},{8,10},{10,8},{12,14},{14,12},{16,18},{18,... | collective-permute-start | bytes 1253384 | tf_op jit(solution)/shard_map/ppermute | solution.py:321
  5.4 3.7 %collective-permute-start.3 = (bf16[544,128]{1,0:T(8,128)(2,1)S(1)}, bf16[544,128]{1,0:T(8,128)(2,1)S(1)}, u32[]{:S(2)}, u32[]{:S(2)}) collective-permute-start(bf16[544,128]{1,0:T(8,128)(2,1)S(1)} %get-tuple-element.34), channel_id=1, source_target_pairs={{0,16},{2,18},{4,20},{6,22},{8,24},{10,26},{12,28},{14,30},{16,0},... | collective-permute-start | bytes 417800 | tf_op jit(solution)/shard_map/ppermute | solution.py:321
  9.1 1.3 %collective-permute-start.4 = (bf16[544,128]{1,0:T(8,128)(2,1)S(1)}, bf16[544,128]{1,0:T(8,128)(2,1)S(1)}, u32[]{:S(2)}, u32[]{:S(2)}) collective-permute-start(bf16[544,128]{1,0:T(8,128)(2,1)S(1)} %get-tuple-element.35), channel_id=1, source_target_pairs={{0,24},{2,26},{4,28},{6,30},{8,16},{10,18},{12,20},{14,22},{16,8},... | collective-permute-start | bytes 417800 | tf_op jit(solution)/shard_map/ppermute | solution.py:321
  10.4 0.0 collective-permute-done.other_ref.refs_1_
  10.4 0.0 copy-start
  10.4 3.2 %rest.1 = (bf16[272,128]{1,0:T(8,128)(2,1)S(1)}, bf16[544,128]{1,0:T(8,128)(2,1)S(1)}, bf16[544,128]{1,0:T(8,128)(2,1)S(1)}, bf16[544,128]{1,0:T(8,128)(2,1)S(1)...) custom-call(s32[1]{0:T(128)} %bitcast.2.me_ref, s32[1,4096]{1,0:T(1,128)S(1)} %get-tuple-element.26.owner_ref, ...), custom_call_target="tpu_custom_call" | custom-call | flops 2147483648 | bytes 2097152 | tf_op jit(solution)/shard_map/rest/pallas_call | solution.py:366
  13.6 1.6 %collective-permute-start.7 = (bf16[544,128]{1,0:T(8,128)(2,1)S(1)}, bf16[544,128]{1,0:T(8,128)(2,1)S(1)}, u32[]{:S(2)}, u32[]{:S(2)}) collective-permute-start(bf16[544,128]{1,0:T(8,128)(2,1)S(1)} %get-tuple-element.38), channel_id=1, source_target_pairs={{0,4},{2,6},{4,0},{6,2},{8,12},{10,14},{12,8},{14,10},{16,20},{18,... | collective-permute-start | bytes 417800 | tf_op jit(solution)/shard_map/ppermute | solution.py:321
  15.2 0.2 collective-permute-start.8
  15.4 0.0 copy-start.1
  15.4 1.8 %collective-permute-start.9 = (bf16[544,128]{1,0:T(8,128)(2,1)S(1)}, bf16[544,128]{1,0:T(8,128)(2,1)S(1)}, u32[]{:S(2)}, u32[]{:S(2)}) collective-permute-start(bf16[544,128]{1,0:T(8,128)(2,1)S(1)} %get-tuple-element.40), channel_id=1, source_target_pairs={{0,12},{2,14},{4,8},{6,10},{8,4},{10,6},{12,0},{14,2},{16,28},{18,... | collective-permute-start | bytes 417800 | tf_op jit(solution)/shard_map/ppermute | solution.py:321
  17.2 2.4 %collective-permute-done.3.refs_2_ = bf16[544,128]{1,0:T(8,128)(2,1)S(1)} collective-permute-done((bf16[544,128]{1,0:T(8,128)(2,1)S(1)}, bf16[544,128]{1,0:T(8,128)(2,1)S(1)}, u32[]{:S(2)}, u32[]{:S(2)}) %collective-permute-start.3) | collective-permute-done | bytes 139296 | tf_op jit(solution)/shard_map/ppermute | solution.py:321
  19.6 0.8 %collective-permute-start.1 = (bf16[544,128]{1,0:T(8,128)(2,1)S(1)}, bf16[544,128]{1,0:T(8,128)(2,1)S(1)}, u32[]{:S(2)}, u32[]{:S(2)}) collective-permute-start(bf16[544,128]{1,0:T(8,128)(2,1)S(1)} %get-tuple-element.31), channel_id=1, source_target_pairs={{0,20},{2,22},{4,16},{6,18},{8,28},{10,30},{12,24},{14,26},{16,4},... | collective-permute-start | bytes 417800 | tf_op jit(solution)/shard_map/ppermute | solution.py:321
  20.3 0.0 collective-permute-done.4.refs_3_
  20.3 3.6 %collective-permute-start.2 = (bf16[544,128]{1,0:T(8,128)(2,1)S(1)}, bf16[544,128]{1,0:T(8,128)(2,1)S(1)}, u32[]{:S(2)}, u32[]{:S(2)}) collective-permute-start(bf16[544,128]{1,0:T(8,128)(2,1)S(1)} %get-tuple-element.32), channel_id=1, source_target_pairs={{0,28},{2,30},{4,24},{6,26},{8,20},{10,22},{12,16},{14,18},{16,12}... | collective-permute-start | bytes 417800 | tf_op jit(solution)/shard_map/ppermute | solution.py:321
  23.9 0.0 copy-done
  23.9 0.0 copy-done.1
  23.9 2.8 %core.5 = (f32[512,256]{1,0:T(8,128)S(1)}, f32[512,256]{1,0:T(8,128)S(1)}, bf16[272,128]{1,0:T(8,128)(2,1)S(1)}, bf16[272,128]{1,0:T(8,128)(2,1)S(1)}) custom-call(s32[1]{0:T(128)} %bitcast.flip_ref, s32[256,128]{1,0:T(8,128)S(1)} %copy-done, bf16[32,128]{1,0:T(8,128)(2,1)S(1)} %bitcast.6, bf16[272,128]{1,0:T(8,128)(2,1)S(1)} %get-tuple-element.33.refs_0_, ...), custom_call_target="tpu_custom_call" | custom-call | flops 1 | bytes 1 | tf_op jit(solution)/shard_map/core/pallas_call | solution.py:284
  26.7 0.0 collective-permute-done.7.refs_0_
  26.7 0.1 collective-permute-start.5
  26.8 0.0 collective-permute-done.8.refs_1_
  26.8 0.5 %collective-permute-start.6 = (bf16[272,128]{1,0:T(8,128)(2,1)S(1)}, bf16[272,128]{1,0:T(8,128)(2,1)S(1)}, u32[]{:S(2)}, u32[]{:S(2)}) collective-permute-start(bf16[272,128]{1,0:T(8,128)(2,1)S(1)} %get-tuple-element.37), channel_id=1, source_target_pairs={{0,2},{2,0},{4,6},{6,4},{8,10},{10,8},{12,14},{14,12},{16,18},{18,... | collective-permute-start | bytes 208904 | tf_op jit(solution)/shard_map/ppermute | solution.py:321
  27.3 0.5 %collective-permute-done.9.refs_2_ = bf16[544,128]{1,0:T(8,128)(2,1)S(1)} collective-permute-done((bf16[544,128]{1,0:T(8,128)(2,1)S(1)}, bf16[544,128]{1,0:T(8,128)(2,1)S(1)}, u32[]{:S(2)}, u32[]{:S(2)}) %collective-permute-start.9) | collective-permute-done | bytes 139296 | tf_op jit(solution)/shard_map/ppermute | solution.py:321
  27.8 4.2 %core.6 = (f32[512,256]{1,0:T(8,128)S(1)}, f32[512,256]{1,0:T(8,128)S(1)}) custom-call(s32[1]{0:T(128)} %bitcast.flip_ref, s32[256,128]{1,0:T(8,128)S(1)} %copy-done, bf16[32,128]{1,0:T(8,128)(2,1)S(1)} %bitcast.7, bf16[544,128]{1,0:T(8,128)(2,1)S(1)} %collective-permute-done.7.refs_0_, ...), custom_call_target="tpu_custom_call", output_to_operand_aliasing={{0}: (6, {}), {1}: (7, {})} | custom-call | flops 1 | bytes 1 | tf_op jit(solution)/shard_map/core/pallas_call | solution.py:284
  32.0 0.0 collective-permute-done.5.refs_0_
  32.1 0.0 collective-permute-done.6.refs_1_
  32.1 1.6 %core.7 = (f32[512,256]{1,0:T(8,128)S(1)}, f32[512,256]{1,0:T(8,128)S(1)}) custom-call(s32[1]{0:T(128)} %bitcast.flip_ref, s32[256,128]{1,0:T(8,128)S(1)} %copy-done, bf16[32,128]{1,0:T(8,128)(2,1)S(1)} %bitcast.8, bf16[272,128]{1,0:T(8,128)(2,1)S(1)} %collective-permute-done.5.refs_0_, ...), custom_call_target="tpu_custom_call", output_to_operand_aliasing={{0}: (5, {}), {1}: (6, {})} | custom-call | flops 1 | bytes 1 | tf_op jit(solution)/shard_map/core/pallas_call | solution.py:284
  33.7 0.2 collective-permute-done.1.refs_0_
  33.9 0.0 collective-permute-done.2.refs_1_
  33.9 1.8 %core.9 = bf16[512,256]{1,0:T(8,128)(2,1)S(1)} custom-call(s32[1]{0:T(128)} %bitcast.flip_ref, s32[256,128]{1,0:T(8,128)S(1)} %copy-done, bf16[32,128]{1,0:T(8,128)(2,1)S(1)} %bitcast.9, bf16[544,128]{1,0:T(8,128)(2,1)S(1)} %collective-permute-done.1.refs_0_, bf16[544,128]{1,0:T(8,128)(2,1)S(1)} %collective-permute-done.2.refs_1_, ...), custom_call_target="tpu_custom_call" | custom-call | flops 1 | bytes 1 | tf_op jit(solution)/shard_map/core/pallas_call | solution.py:284
  35.6 1.7 %collective-permute-start.10 = (bf16[512,256]{1,0:T(8,128)(2,1)S(1)}, bf16[512,256]{1,0:T(8,128)(2,1)S(1)}, u32[]{:S(2)}, u32[]{:S(2)}) collective-permute-start(bf16[512,256]{1,0:T(8,128)(2,1)S(1)} %core.9), channel_id=1, source_target_pairs={{0,1},{1,0},{2,3},{3,2},{4,5},{5,4},{6,7},{7,6},{8,9},{9,8},{10,11... | collective-permute-start | bytes 786440 | tf_op jit(solution)/shard_map/ppermute | solution.py:395
  37.4 1.9 %core.8.keep_ref = f32[512,256]{1,0:T(8,128)S(1)} custom-call(s32[1]{0:T(128)} %bitcast.flip_ref, s32[256,128]{1,0:T(8,128)S(1)} %copy-done, bf16[32,128]{1,0:T(8,128)(2,1)S(1)} %bitcast.10, bf16[544,128]{1,0:T(8,128)(2,1)S(1)} %collective-permute-done.1.refs_0_, ...), custom_call_target="tpu_custom_call", output_to_operand_aliasing={{}: (5, {})} | custom-call | flops 1 | bytes 1 | tf_op jit(solution)/shard_map/core/pallas_call | solution.py:284
  39.3 4.5 %collective-permute-done.10.got_ref = bf16[512,256]{1,0:T(8,128)(2,1)S(1)} collective-permute-done((bf16[512,256]{1,0:T(8,128)(2,1)S(1)}, bf16[512,256]{1,0:T(8,128)(2,1)S(1)}, u32[]{:S(2)}, u32[]{:S(2)}) %collective-permute-start.10) | collective-permute-done | bytes 262176 | tf_op jit(solution)/shard_map/ppermute | solution.py:395
  43.7 1.2 %finish.1 = bf16[128,1024]{1,0:T(8,128)(2,1)} custom-call(f32[512,256]{1,0:T(8,128)S(1)} %core.8.keep_ref, bf16[512,256]{1,0:T(8,128)(2,1)S(1)} %collective-permute-done.10.got_ref), custom_call_target="tpu_custom_call" | custom-call | tf_op jit(solution)/shard_map/finish/pallas_call | solution.py:397
Async XLA Ops:
  4.9 5.5 %collective-permute-start = (bf16[1632,128]{1,0:T(8,128)(2,1)S(1)}, bf16[1632,128]{1,0:T(8,128)(2,1)S(1)}, u32[]{:S(2)}, u32[]{:S(2)}) collective-permute-start(bf16[1632,128]{1,0:T(8,128)(2,1)S(1)} %get-tuple-element.30), channel_id=1, source_target_pairs={{0,2},{2,0},{4,6},{6,4},{8,10},{10,8},{12,14},{14,12},{16,18},{18,... | collective-permute-start | bytes 1253384 | tf_op jit(solution)/shard_map/ppermute | solution.py:321
  5.4 14.2 %collective-permute-start.3 = (bf16[544,128]{1,0:T(8,128)(2,1)S(1)}, bf16[544,128]{1,0:T(8,128)(2,1)S(1)}, u32[]{:S(2)}, u32[]{:S(2)}) collective-permute-start(bf16[544,128]{1,0:T(8,128)(2,1)S(1)} %get-tuple-element.34), channel_id=1, source_target_pairs={{0,16},{2,18},{4,20},{6,22},{8,24},{10,26},{12,28},{14,30},{16,0},... | collective-permute-start | bytes 417800 | tf_op jit(solution)/shard_map/ppermute | solution.py:321
  9.1 11.3 %collective-permute-start.4 = (bf16[544,128]{1,0:T(8,128)(2,1)S(1)}, bf16[544,128]{1,0:T(8,128)(2,1)S(1)}, u32[]{:S(2)}, u32[]{:S(2)}) collective-permute-start(bf16[544,128]{1,0:T(8,128)(2,1)S(1)} %get-tuple-element.35), channel_id=1, source_target_pairs={{0,24},{2,26},{4,28},{6,30},{8,16},{10,18},{12,20},{14,22},{16,8},... | collective-permute-start | bytes 417800 | tf_op jit(solution)/shard_map/ppermute | solution.py:321
  10.4 13.5 %copy-start = (s32[256,128]{1,0:T(8,128)S(1)}, s32[256,128]{1,0:T(8,128)}, u32[]{:S(2)}) copy-start(s32[256,128]{1,0:T(8,128)} %sampled_ref.9) | copy-start | bytes 393220
  13.6 13.1 %collective-permute-start.7 = (bf16[544,128]{1,0:T(8,128)(2,1)S(1)}, bf16[544,128]{1,0:T(8,128)(2,1)S(1)}, u32[]{:S(2)}, u32[]{:S(2)}) collective-permute-start(bf16[544,128]{1,0:T(8,128)(2,1)S(1)} %get-tuple-element.38), channel_id=1, source_target_pairs={{0,4},{2,6},{4,0},{6,2},{8,12},{10,14},{12,8},{14,10},{16,20},{18,... | collective-permute-start | bytes 417800 | tf_op jit(solution)/shard_map/ppermute | solution.py:321
  15.2 11.7 %collective-permute-start.8 = (bf16[544,128]{1,0:T(8,128)(2,1)S(1)}, bf16[544,128]{1,0:T(8,128)(2,1)S(1)}, u32[]{:S(2)}, u32[]{:S(2)}) collective-permute-start(bf16[544,128]{1,0:T(8,128)(2,1)S(1)} %get-tuple-element.39), channel_id=1, source_target_pairs={{0,8},{2,10},{4,12},{6,14},{8,0},{10,2},{12,4},{14,6},{16,24},{18,... | collective-permute-start | bytes 417800 | tf_op jit(solution)/shard_map/ppermute | solution.py:321
  15.4 8.5 %copy-start.1 = (bf16[128,32]{0,1:T(8,128)(2,1)S(1)}, bf16[128,32]{0,1:T(8,128)(2,1)}, u32[]{:S(2)}) copy-start(bf16[128,32]{0,1:T(8,128)(2,1)} %param.11) | copy-start | bytes 24580
  15.4 12.4 %collective-permute-start.9 = (bf16[544,128]{1,0:T(8,128)(2,1)S(1)}, bf16[544,128]{1,0:T(8,128)(2,1)S(1)}, u32[]{:S(2)}, u32[]{:S(2)}) collective-permute-start(bf16[544,128]{1,0:T(8,128)(2,1)S(1)} %get-tuple-element.40), channel_id=1, source_target_pairs={{0,12},{2,14},{4,8},{6,10},{8,4},{10,6},{12,0},{14,2},{16,28},{18,... | collective-permute-start | bytes 417800 | tf_op jit(solution)/shard_map/ppermute | solution.py:321
  19.6 14.3 %collective-permute-start.1 = (bf16[544,128]{1,0:T(8,128)(2,1)S(1)}, bf16[544,128]{1,0:T(8,128)(2,1)S(1)}, u32[]{:S(2)}, u32[]{:S(2)}) collective-permute-start(bf16[544,128]{1,0:T(8,128)(2,1)S(1)} %get-tuple-element.31), channel_id=1, source_target_pairs={{0,20},{2,22},{4,16},{6,18},{8,28},{10,30},{12,24},{14,26},{16,4},... | collective-permute-start | bytes 417800 | tf_op jit(solution)/shard_map/ppermute | solution.py:321
  20.3 13.5 %collective-permute-start.2 = (bf16[544,128]{1,0:T(8,128)(2,1)S(1)}, bf16[544,128]{1,0:T(8,128)(2,1)S(1)}, u32[]{:S(2)}, u32[]{:S(2)}) collective-permute-start(bf16[544,128]{1,0:T(8,128)(2,1)S(1)} %get-tuple-element.32), channel_id=1, source_target_pairs={{0,28},{2,30},{4,24},{6,26},{8,20},{10,22},{12,16},{14,18},{16,12}... | collective-permute-start | bytes 417800 | tf_op jit(solution)/shard_map/ppermute | solution.py:321
  26.7 5.3 %collective-permute-start.5 = (bf16[272,128]{1,0:T(8,128)(2,1)S(1)}, bf16[272,128]{1,0:T(8,128)(2,1)S(1)}, u32[]{:S(2)}, u32[]{:S(2)}) collective-permute-start(bf16[272,128]{1,0:T(8,128)(2,1)S(1)} %get-tuple-element.36), channel_id=1, source_target_pairs={{0,2},{2,0},{4,6},{6,4},{8,10},{10,8},{12,14},{14,12},{16,18},{18,... | collective-permute-start | bytes 208904 | tf_op jit(solution)/shard_map/ppermute | solution.py:321
  26.8 5.2 %collective-permute-start.6 = (bf16[272,128]{1,0:T(8,128)(2,1)S(1)}, bf16[272,128]{1,0:T(8,128)(2,1)S(1)}, u32[]{:S(2)}, u32[]{:S(2)}) collective-permute-start(bf16[272,128]{1,0:T(8,128)(2,1)S(1)} %get-tuple-element.37), channel_id=1, source_target_pairs={{0,2},{2,0},{4,6},{6,4},{8,10},{10,8},{12,14},{14,12},{16,18},{18,... | collective-permute-start | bytes 208904 | tf_op jit(solution)/shard_map/ppermute | solution.py:321
  35.6 8.1 %collective-permute-start.10 = (bf16[512,256]{1,0:T(8,128)(2,1)S(1)}, bf16[512,256]{1,0:T(8,128)(2,1)S(1)}, u32[]{:S(2)}, u32[]{:S(2)}) collective-permute-start(bf16[512,256]{1,0:T(8,128)(2,1)S(1)} %core.9), channel_id=1, source_target_pairs={{0,1},{1,0},{2,3},{3,2},{4,5},{5,4},{6,7},{7,6},{8,9},{9,8},{10,11... | collective-permute-start | bytes 786440 | tf_op jit(solution)/shard_map/ppermute | solution.py:395
